TPU v7x, 32 devices: a whole 2x2x4 slice. The times are simulated.
32 devices in a mesh: dp: 8 (over z, x), seq: 4 (over y, core).
Axes of the slice: x: 2, y: 2, z: 4, core: 2. Of those that a mesh axis runs over, the one named last changes fastest.
Arguments:
- inputs: bfloat16 [8, 1024, 1280], P('dp', 'seq'), may hold values from -6 to 6
- lengths: int32 [8], P('dp'), may hold values from 256 to 1024, as said below
- cotangent: bfloat16 [8, 1024, 1280], P('dp', 'seq'), may hold values from -6 to 6
- gain_attn: bfloat16 [1280], P(('dp', 'seq')), may hold values from 0.099609375 to 1.8984375
- w_query: bfloat16 [1280, 1280], P(('dp', 'seq')), may hold values from -0.15625 to 0.15625
- bias_query: bfloat16 [1280], P(('dp', 'seq')), may hold values from -3 to 3
- query_scale: bfloat16 [1280], P(('dp', 'seq')), may hold values from -3 to 3
- w_key: bfloat16 [1280, 1280], P(('dp', 'seq')), may hold values from -0.15625 to 0.15625
- w_value: bfloat16 [1280, 1280], P(('dp', 'seq')), may hold values from -0.15625 to 0.15625
- bias_value: bfloat16 [1280], P(('dp', 'seq')), may hold values from -3 to 3
- w_out: bfloat16 [1280, 1280], P(('dp', 'seq')), may hold values from -1.25 to 1.25
- gain_mlp: bfloat16 [1280], P(('dp', 'seq')), may hold values from 0.099609375 to 1.8984375
- w_hidden: bfloat16 [1280, 1280], P(('dp', 'seq')), may hold values from -0.15625 to 0.15625
- w_back: bfloat16 [1280, 1280], P(('dp', 'seq')), may hold values from -0.15625 to 0.15625
Outputs:
- outputs: bfloat16 [8, 1024, 1280], P('dp', 'seq')
- input_grad: float32 [8, 1024, 1280], P('dp', 'seq')
- grad_gain_attn: float32 [1280], P(('dp', 'seq'))
- grad_w_query: float32 [1280, 1280], P(('dp', 'seq'))
- grad_bias_query: float32 [1280], P(('dp', 'seq'))
- grad_query_scale: float32 [1280], P(('dp', 'seq'))
- grad_w_key: float32 [1280, 1280], P(('dp', 'seq'))
- grad_w_value: float32 [1280, 1280], P(('dp', 'seq'))
- grad_bias_value: float32 [1280], P(('dp', 'seq'))
- grad_w_out: float32 [1280, 1280], P(('dp', 'seq'))
- grad_gain_mlp: float32 [1280], P(('dp', 'seq'))
- grad_w_hidden: float32 [1280, 1280], P(('dp', 'seq'))
- grad_w_back: float32 [1280, 1280], P(('dp', 'seq'))
Inputs may be any that keep to these rules, and one draw needn't show every extreme that they name: Slots from lengths[b] on are padding; some sequence has exactly 1024 valid slots and some exactly 256.
All inputs are finite; a program needn't handle non-finite values.
Results may differ from a plain program's by a relative error of at most 0.015.
Values may be sent and summed in bfloat16 or wider, within the bound.
A program may use at most 192 MiB of HBM per device.

v0:
```python
import math

import jax
import jax.numpy as jnp
from jax import lax
from jax.sharding import PartitionSpec as P

HEADS = 16
HEAD_DIM = 80


query_gain = 1.442695041
masked_score = -1e30


def normed(values):
    squares = jnp.mean(values * values, axis=-1, keepdims=True)
    inverse = lax.rsqrt(squares + 1e-06)
    return (values * inverse, inverse)


def norm_back(grad_in, unit, inverse, gain):
    scaled = grad_in * gain
    return inverse * (scaled - unit * jnp.mean(scaled * unit, axis=-1, keepdims=True))


def row_product(left, right):
    return lax.dot_general(
        left, right, (((0,), (0,)), ((), ())), preferred_element_type=jnp.float32
    )


def back_product(left, right):
    return lax.dot_general(
        left, right, (((1,), (1,)), ((), ())), preferred_element_type=jnp.float32
    )


def shards(
    inputs,
    lengths,
    cotangent,
    gain_attn,
    w_query,
    bias_query,
    query_scale,
    w_key,
    w_value,
    bias_value,
    w_out,
    gain_mlp,
    w_hidden,
    w_back,
):
    seq_dev, group_rows, width = inputs.shape
    tok_rows = seq_dev * group_rows
    head_count = HEADS
    head_width = HEAD_DIM
    gathered = (
        lax.all_gather(gain_attn, ("dp", "seq"), axis=0, tiled=True),
        lax.all_gather(w_query, ("dp", "seq"), axis=0, tiled=True),
        lax.all_gather(bias_query, ("dp", "seq"), axis=0, tiled=True),
        lax.all_gather(query_scale, ("dp", "seq"), axis=0, tiled=True),
        lax.all_gather(w_key, ("dp", "seq"), axis=0, tiled=True),
        lax.all_gather(w_value, ("dp", "seq"), axis=0, tiled=True),
        lax.all_gather(bias_value, ("dp", "seq"), axis=0, tiled=True),
        lax.all_gather(w_out, ("dp", "seq"), axis=0, tiled=True),
        lax.all_gather(gain_mlp, ("dp", "seq"), axis=0, tiled=True),
        lax.all_gather(w_hidden, ("dp", "seq"), axis=0, tiled=True),
        lax.all_gather(w_back, ("dp", "seq"), axis=0, tiled=True),
    )
    (
        norm_one,
        query_mat,
        query_bias,
        query_log,
        key_mat,
        value_mat,
        value_bias,
        output_mat,
        norm_two,
        hidden_mat,
        back_mat,
    ) = gathered
    ff_width = hidden_mat.shape[1]
    offset = lax.axis_index("seq") * group_rows
    place = offset + jnp.arange(group_rows, dtype=jnp.int32)
    valid = place[None, :] < lengths[:, None]
    row_valid = valid.reshape(tok_rows, 1)
    inputs_rows = inputs.reshape(tok_rows, width).astype(jnp.float32)
    unit_one, inverse_one = normed(inputs_rows)
    gain_one = norm_one.astype(jnp.float32)
    normed_one = (unit_one * gain_one).astype(jnp.bfloat16)
    query_raw = jnp.dot(
        normed_one, query_mat, preferred_element_type=jnp.float32
    ) + query_bias.astype(jnp.float32)
    query_logf = query_log.astype(jnp.float32)
    scale_vec = jax.nn.softplus(query_logf) * (query_gain / math.sqrt(head_width))
    queries = (query_raw * scale_vec).astype(jnp.bfloat16)
    keys_local = jnp.dot(normed_one, key_mat, preferred_element_type=jnp.float32).astype(
        jnp.bfloat16
    )
    values_local = (
        jnp.dot(normed_one, value_mat, preferred_element_type=jnp.float32)
        + value_bias.astype(jnp.float32)
    ).astype(jnp.bfloat16)
    keys_three = keys_local.reshape(seq_dev, group_rows, width)
    values_three = values_local.reshape(seq_dev, group_rows, width)
    queries_three = queries.reshape(seq_dev, group_rows, width)
    keys_all, values_all = (
        lax.all_gather(keys_three, "seq", axis=1, tiled=True),
        lax.all_gather(values_three, "seq", axis=1, tiled=True),
    )
    seq_slots = keys_all.shape[1]
    key_place = jnp.arange(seq_slots, dtype=jnp.int32)
    allowed = key_place[None, :] <= place[:, None]

    def attend(pieces):
        query_block, key_block, value_block = pieces
        query_heads = query_block.reshape(group_rows, head_count, head_width)
        key_heads = key_block.reshape(seq_slots, head_count, head_width)
        value_heads = value_block.reshape(seq_slots, head_count, head_width)
        scores = jnp.einsum(
            "qhd,khd->hqk", query_heads, key_heads, preferred_element_type=jnp.float32
        )
        scores = jnp.where(allowed[None], scores, masked_score)
        largest = jnp.max(scores, axis=-1, keepdims=True)
        raised = jnp.exp(scores - largest)
        totals = jnp.sum(raised, axis=-1, keepdims=True)
        weights_soft = (raised / totals).astype(jnp.bfloat16)
        mixed = jnp.einsum(
            "hqk,khd->qhd", weights_soft, value_heads, preferred_element_type=jnp.float32
        )
        log_total = largest[..., 0] + jnp.log(totals[..., 0])
        return (mixed.reshape(group_rows, width).astype(jnp.bfloat16), log_total)

    mixed_three, log_totals = lax.map(attend, (queries_three, keys_all, values_all))
    mixed = mixed_three.reshape(tok_rows, width)
    middle = inputs_rows + jnp.dot(mixed, output_mat, preferred_element_type=jnp.float32)
    unit_two, inverse_two = normed(middle)
    gain_two = norm_two.astype(jnp.float32)
    normed_two = (unit_two * gain_two).astype(jnp.bfloat16)
    hidden = jnp.dot(normed_two, hidden_mat, preferred_element_type=jnp.float32)
    active = jax.nn.silu(hidden).astype(jnp.bfloat16)
    result = middle + jnp.dot(active, back_mat, preferred_element_type=jnp.float32)
    outputs = (
        jnp.where(row_valid, result, 0.0).astype(jnp.bfloat16).reshape(seq_dev, group_rows, width)
    )
    again = (
        lax.all_gather(gain_attn, ("dp", "seq"), axis=0, tiled=True),
        lax.all_gather(w_query, ("dp", "seq"), axis=0, tiled=True),
        lax.all_gather(w_key, ("dp", "seq"), axis=0, tiled=True),
        lax.all_gather(w_value, ("dp", "seq"), axis=0, tiled=True),
        lax.all_gather(w_out, ("dp", "seq"), axis=0, tiled=True),
        lax.all_gather(gain_mlp, ("dp", "seq"), axis=0, tiled=True),
        lax.all_gather(w_hidden, ("dp", "seq"), axis=0, tiled=True),
        lax.all_gather(w_back, ("dp", "seq"), axis=0, tiled=True),
    )
    norm_one, query_mat, key_mat, value_mat, output_mat, norm_two, hidden_mat, back_mat = again
    gain_one = norm_one.astype(jnp.float32)
    gain_two = norm_two.astype(jnp.float32)
    keys_back, values_back = (
        lax.all_gather(keys_three, "seq", axis=1, tiled=True),
        lax.all_gather(values_three, "seq", axis=1, tiled=True),
    )
    cot_rows = cotangent.reshape(tok_rows, width)
    grad_out = jnp.where(row_valid, cot_rows, jnp.zeros_like(cot_rows))
    grad_active = back_product(grad_out, back_mat)
    sigma = jax.nn.sigmoid(hidden)
    grad_hidden = (grad_active * sigma * (1.0 + hidden * (1.0 - sigma))).astype(jnp.bfloat16)
    grad_normed_two = back_product(grad_hidden, hidden_mat)
    grad_gain_two = jnp.sum(grad_normed_two * unit_two, axis=0)
    grad_middle = grad_out.astype(jnp.float32) + norm_back(
        grad_normed_two, unit_two, inverse_two, gain_two
    )
    grad_middle_low = grad_middle.astype(jnp.bfloat16)
    grad_mixed = back_product(grad_middle_low, output_mat).astype(jnp.bfloat16)
    grad_mixed_three = grad_mixed.reshape(seq_dev, group_rows, width)

    def attend_query(pieces):
        query_block, key_block, value_block, grad_block, log_total = pieces
        query_heads = query_block.reshape(group_rows, head_count, head_width)
        key_heads = key_block.reshape(seq_slots, head_count, head_width)
        value_heads = value_block.reshape(seq_slots, head_count, head_width)
        grad_heads = grad_block.reshape(group_rows, head_count, head_width)
        scores = jnp.einsum(
            "qhd,khd->hqk", query_heads, key_heads, preferred_element_type=jnp.float32
        )
        scores = jnp.where(allowed[None], scores, masked_score)
        weights_soft = jnp.exp(scores - log_total[..., None])
        grad_soft = jnp.einsum(
            "qhd,khd->hqk", grad_heads, value_heads, preferred_element_type=jnp.float32
        )
        inner = jnp.sum(weights_soft * grad_soft, axis=-1, keepdims=True)
        grad_scores = (weights_soft * (grad_soft - inner)).astype(jnp.bfloat16)
        grad_queries = jnp.einsum(
            "hqk,khd->qhd", grad_scores, key_heads, preferred_element_type=jnp.float32
        )
        return (grad_queries.reshape(group_rows, width), inner[..., 0])

    grad_queries, inner_rows = lax.map(
        attend_query, (queries_three, keys_back, values_back, grad_mixed_three, log_totals)
    )
    queries_every, grad_every = (
        lax.all_gather(queries_three, "seq", axis=1, tiled=True),
        lax.all_gather(grad_mixed_three, "seq", axis=1, tiled=True),
    )
    lse_every, inner_every = (
        lax.all_gather(log_totals, "seq", axis=2, tiled=True),
        lax.all_gather(inner_rows, "seq", axis=2, tiled=True),
    )
    later = key_place[:, None] >= place[None, :]

    def key_side(pieces):
        query_block, grad_block, key_block, value_block, lse_block, inner_block = pieces
        query_heads = query_block.reshape(seq_slots, head_count, head_width)
        grad_heads = grad_block.reshape(seq_slots, head_count, head_width)
        key_heads = key_block.reshape(group_rows, head_count, head_width)
        value_heads = value_block.reshape(group_rows, head_count, head_width)
        scores = jnp.einsum(
            "qhd,khd->hqk", query_heads, key_heads, preferred_element_type=jnp.float32
        )
        scores = jnp.where(later[None], scores, masked_score)
        weights_soft = jnp.exp(scores - lse_block[..., None])
        weights_low = weights_soft.astype(jnp.bfloat16)
        grad_soft = jnp.einsum(
            "qhd,khd->hqk", grad_heads, value_heads, preferred_element_type=jnp.float32
        )
        grad_scores = (weights_soft * (grad_soft - inner_block[..., None])).astype(jnp.bfloat16)
        grad_keys = jnp.einsum(
            "hqk,qhd->khd", grad_scores, query_heads, preferred_element_type=jnp.float32
        )
        grad_values = jnp.einsum(
            "hqk,qhd->khd", weights_low, grad_heads, preferred_element_type=jnp.float32
        )
        return (grad_keys.reshape(group_rows, width), grad_values.reshape(group_rows, width))

    grad_keys_sum, grad_values_sum = lax.map(
        key_side, (queries_every, grad_every, keys_three, values_three, lse_every, inner_every)
    )
    grad_keys = grad_keys_sum.reshape(tok_rows, width).astype(jnp.bfloat16)
    grad_values = grad_values_sum.reshape(tok_rows, width).astype(jnp.bfloat16)
    grad_queries = grad_queries.reshape(tok_rows, width)
    grad_query_raw = (grad_queries * scale_vec).astype(jnp.bfloat16)
    grad_scale = jnp.sum(grad_queries * query_raw, axis=0)
    grad_query_log = grad_scale * jax.nn.sigmoid(query_logf) * (query_gain / math.sqrt(head_width))
    grad_query_bias = jnp.sum(grad_query_raw.astype(jnp.float32), axis=0)
    grad_value_bias = jnp.sum(grad_values.astype(jnp.float32), axis=0)
    grad_normed_one = (
        back_product(grad_query_raw, query_mat)
        + back_product(grad_keys, key_mat)
        + back_product(grad_values, value_mat)
    )
    grad_gain_one = jnp.sum(grad_normed_one * unit_one, axis=0)
    input_grad = grad_middle + norm_back(grad_normed_one, unit_one, inverse_one, gain_one)
    dp_count = lax.axis_size("dp")
    seq_count = lax.axis_size("seq")
    share = width // (dp_count * seq_count)
    share_ff = ff_width // (dp_count * seq_count)
    left_parts = (
        lax.all_to_all(
            normed_one.reshape(tok_rows, dp_count, seq_count, share),
            "seq",
            split_axis=2,
            concat_axis=0,
            tiled=True,
        ),
        lax.all_to_all(
            mixed.reshape(tok_rows, dp_count, seq_count, share),
            "seq",
            split_axis=2,
            concat_axis=0,
            tiled=True,
        ),
        lax.all_to_all(
            normed_two.reshape(tok_rows, dp_count, seq_count, share),
            "seq",
            split_axis=2,
            concat_axis=0,
            tiled=True,
        ),
        lax.all_to_all(
            active.reshape(tok_rows, dp_count, seq_count, share_ff),
            "seq",
            split_axis=2,
            concat_axis=0,
            tiled=True,
        ),
    )
    left_normed_one = left_parts[0].reshape(-1, dp_count * share)
    left_mixed = left_parts[1].reshape(-1, dp_count * share)
    left_normed_two = left_parts[2].reshape(-1, dp_count * share)
    left_active = left_parts[3].reshape(-1, dp_count * share_ff)
    right_parts = (
        lax.all_gather(grad_query_raw, "seq", axis=0, tiled=True),
        lax.all_gather(grad_keys, "seq", axis=0, tiled=True),
        lax.all_gather(grad_values, "seq", axis=0, tiled=True),
        lax.all_gather(grad_middle_low, "seq", axis=0, tiled=True),
        lax.all_gather(grad_hidden, "seq", axis=0, tiled=True),
        lax.all_gather(grad_out, "seq", axis=0, tiled=True),
    )
    right_query, right_keys, right_values, right_middle, right_hidden, right_out = right_parts
    part_query_mat = row_product(left_normed_one, right_query)
    part_key_mat = row_product(left_normed_one, right_keys)
    part_value_mat = row_product(left_normed_one, right_values)
    part_output_mat = row_product(left_mixed, right_middle)
    part_hidden_mat = row_product(left_normed_two, right_hidden)
    part_back_mat = row_product(left_active, right_out)
    matrices = (
        lax.psum_scatter(
            part_query_mat.astype(jnp.bfloat16), "dp", scatter_dimension=0, tiled=True
        ).astype(jnp.float32),
        lax.psum_scatter(
            part_key_mat.astype(jnp.bfloat16), "dp", scatter_dimension=0, tiled=True
        ).astype(jnp.float32),
        lax.psum_scatter(
            part_value_mat.astype(jnp.bfloat16), "dp", scatter_dimension=0, tiled=True
        ).astype(jnp.float32),
        lax.psum_scatter(
            part_output_mat.astype(jnp.bfloat16), "dp", scatter_dimension=0, tiled=True
        ).astype(jnp.float32),
        lax.psum_scatter(
            part_hidden_mat.astype(jnp.bfloat16), "dp", scatter_dimension=0, tiled=True
        ).astype(jnp.float32),
        lax.psum_scatter(
            part_back_mat.astype(jnp.bfloat16), "dp", scatter_dimension=0, tiled=True
        ).astype(jnp.float32),
    )
    vectors = (
        lax.psum_scatter(grad_gain_one, ("dp", "seq"), scatter_dimension=0, tiled=True),
        lax.psum_scatter(grad_query_bias, ("dp", "seq"), scatter_dimension=0, tiled=True),
        lax.psum_scatter(grad_query_log, ("dp", "seq"), scatter_dimension=0, tiled=True),
        lax.psum_scatter(grad_value_bias, ("dp", "seq"), scatter_dimension=0, tiled=True),
        lax.psum_scatter(grad_gain_two, ("dp", "seq"), scatter_dimension=0, tiled=True),
    )
    return (
        outputs,
        input_grad.reshape(seq_dev, group_rows, width),
        vectors[0],
        matrices[0],
        vectors[1],
        vectors[2],
        matrices[1],
        matrices[2],
        vectors[3],
        matrices[3],
        vectors[4],
        matrices[4],
        matrices[5],
    )


def solution(mesh):
    placed = (
        P("dp", "seq", None),
        P("dp"),
        P("dp", "seq", None),
        P(("dp", "seq")),
        P(("dp", "seq"), None),
        P(("dp", "seq")),
        P(("dp", "seq")),
        P(("dp", "seq"), None),
        P(("dp", "seq"), None),
        P(("dp", "seq")),
        P(("dp", "seq"), None),
        P(("dp", "seq")),
        P(("dp", "seq"), None),
        P(("dp", "seq"), None),
    )
    return jax.shard_map(
        shards,
        mesh=mesh,
        in_specs=placed,
        out_specs=(
            P("dp", "seq", None),
            P("dp", "seq", None),
            P(("dp", "seq")),
            P(("dp", "seq"), None),
            P(("dp", "seq")),
            P(("dp", "seq")),
            P(("dp", "seq"), None),
            P(("dp", "seq"), None),
            P(("dp", "seq")),
            P(("dp", "seq"), None),
            P(("dp", "seq")),
            P(("dp", "seq"), None),
            P(("dp", "seq"), None),
        ),
        check_vma=False,
    )
```

profile of v0, /device:TPU:0, one launch (start us, length us, event | category | flops | bytes accessed | tf_op | source)
XLA Modules:
  0.0 1029.4 jit_solution(17642460554471393835)
XLA Ops:
  13.7 42.5 %all-reduce.11 = (bf16[1280]{0:T(1024)(128)(2,1)S(1)}, bf16[1280]{0:T(1024)(128)(2,1)S(1)}, bf16[1280]{0:T(1024)(128)(2,1)S(1)}, bf16[1280]{0:T(1024)(128)(2,1)S(1)}, bf16[1280]{0:T(1024)(128)(2,1)S(1)}) all-reduce(bf16[1280]{0:T(1024)(128)(2,1)S(1)} %dynamic-update-slice.1, ...), channel_id=1, replica_groups=mesh['dp'=8,'seq'=4] {'dp','seq'}, use_global_device_ids=true, to_apply=%add.1 | all-reduce | flops 6400 | bytes 25600
  57.6 15.5 %all-gather.27.cloned.1.call-done = bf16[1280,1280]{1,0:T(8,128)(2,1)} async-done(((bf16[40,1280]{1,0:T(8,128)(2,1)}), bf16[1280,1280]{1,0:T(8,128)(2,1)}) %all-gather.27.cloned.1.call-update) | async-done | bytes 3276816 | tf_op jit(solution)/shard_map/all_gather | solution.py:64
  77.2 56.9 %all-gather.23.cloned.1.call-done = bf16[1280,1280]{1,0:T(8,128)(2,1)} async-done(((bf16[40,1280]{1,0:T(8,128)(2,1)}), bf16[1280,1280]{1,0:T(8,128)(2,1)}) %all-gather.23.cloned.1.call-update) | async-done | bytes 3276816 | tf_op jit(solution)/shard_map/all_gather | solution.py:65
  142.7 52.5 %all-gather.25.cloned.1.call-done = bf16[1280,1280]{1,0:T(8,128)(2,1)} async-done(((bf16[40,1280]{1,0:T(8,128)(2,1)}), bf16[1280,1280]{1,0:T(8,128)(2,1)}) %all-gather.25.cloned.1.call-update) | async-done | bytes 3276816 | tf_op jit(solution)/shard_map/all_gather | solution.py:61
  200.9 20.2 %all-gather.49.cloned.1.call-done = bf16[1024,1280]{1,0:T(8,128)(2,1)} async-done(((bf16[256,1280]{1,0:T(8,128)(2,1)}), bf16[1024,1280]{1,0:T(8,128)(2,1)}) %all-gather.49.cloned.1.call-update) | async-done | bytes 2621456 | tf_op jit(solution)/shard_map/all_gather | solution.py:111
  238.9 9.8 all-gather.47.cloned.1.call-done
  253.1 9.5 fusion.17
  262.7 48.1 %all-gather.29.cloned.1.call-done = bf16[1280,1280]{1,0:T(8,128)(2,1)} async-done(((bf16[40,1280]{1,0:T(8,128)(2,1)}), bf16[1280,1280]{1,0:T(8,128)(2,1)}) %all-gather.29.cloned.1.call-update) | async-done | bytes 3276816 | tf_op jit(solution)/shard_map/all_gather | solution.py:67
  316.2 55.7 %all-gather.31.cloned.1.call-done = bf16[1280,1280]{1,0:T(8,128)(2,1)} async-done(((bf16[40,1280]{1,0:T(8,128)(2,1)}), bf16[1280,1280]{1,0:T(8,128)(2,1)}) %all-gather.31.cloned.1.call-update) | async-done | bytes 3276816 | tf_op jit(solution)/shard_map/all_gather | solution.py:69
  376.3 56.6 %all-gather.33.cloned.1.call-done = bf16[1280,1280]{1,0:T(8,128)(2,1)} async-done(((bf16[40,1280]{1,0:T(8,128)(2,1)}), bf16[1280,1280]{1,0:T(8,128)(2,1)}) %all-gather.33.cloned.1.call-update) | async-done | bytes 3276816 | tf_op jit(solution)/shard_map/all_gather | solution.py:70
  453.0 13.9 %multiply_reduce_fusion = (f32[16,256]{1,0:T(8,128)}, f32[16,256,1024]{2,1,0:T(8,128)}) fusion(f32[16,256,1024]{2,1,0:T(8,128)} %copy-done, f32[16,256]{1,0:T(8,128)S(1)} %log_add_fusion, pred[256,1024]{1,0:T(8,128)(4,1)S(1)} %iota_compare_fusion.1, bf16[256,16,80]{0,2,1:T(8,128)(2,1)} %bitcast.162, bf16[1024,16,80]{0,2,1:T(8,128)(2,1)} %bitcast.143), kind=kOutput, calls=%fused_computation.3 | convolution fusion | flops 687861760 | bytes 37126144 | tf_op jit(solution)/shard_map/while/body/eval_jaxpr/qhd,khd->hqk/dot_general | solution.py:191
  467.0 15.2 %convert_reduce_fusion.1 = (f32[16,80]{1,0:T(8,128)}, f32[16,80,256]{2,1,0:T(8,128)}) fusion(f32[16,80]{1,0:T(8,128)} %mul.201, bf16[1024,16,80]{0,2,1:T(8,128)(2,1)S(1)} %bitcast.139, f32[16,256,1024]{2,1,0:T(8,128)} %get-tuple-element.117, f32[16,256,1024]{2,1,0:T(8,128)} %copy-done, f32[16,256]{1,0:T(8,128)} %get-tuple-element.116, ...), kind=kOutput, calls=%fused_computation.50 | convolution fusion | flops 693369600 | bytes 37791744 | tf_op jit(solution)/shard_map/while/body/eval_jaxpr/hqk,khd->qhd/dot_general | solution.py:196
  521.5 12.4 %fusion.21 = bf16[16,80,256]{2,1,0:T(8,128)(2,1)} fusion(bf16[1024,16,80]{0,2,1:T(8,128)(2,1)S(1)} %bitcast.141, f32[16,1024,256]{2,1,0:T(8,128)} %fusion.40, bf16[1024,16,80]{0,2,1:T(8,128)(2,1)} %bitcast.150, bf16[256,16,80]{0,2,1:T(8,128)(2,1)} %bitcast.170, f32[16,1024]{1,0:T(8,128)} %all-gather.5, f32[16,1024]{1,0:T(8,128)} %all-gather.3, ...), kind=kOutput, calls=%fused_computation.41 | convolution fusion | flops 1363476480 | bytes 23724032 | tf_op jit(solution)/shard_map/while/body/eval_jaxpr/hqk,qhd->khd/dot_general | solution.py:230
  535.3 12.7 %all_to_all.60 = bf16[256,8,4,40]{0,3,1,2:T(8,128)(2,1)S(1)} all-to-all(bf16[256,8,4,40]{0,3,1,2:T(8,128)(2,1)S(1)} %copy.74), channel_id=1, replica_groups=mesh['dp'=8,'seq'=4] {'seq'}, dimensions={2} | all-to-all | bytes 1310720 | tf_op jit(solution)/shard_map/all_to_all | solution.py:282
  564.2 12.7 %all_to_all.61 = bf16[256,8,4,40]{0,3,1,2:T(8,128)(2,1)S(1)} all-to-all(bf16[256,8,4,40]{0,3,1,2:T(8,128)(2,1)S(1)} %copy.65), channel_id=1, replica_groups=mesh['dp'=8,'seq'=4] {'seq'}, dimensions={2} | all-to-all | bytes 1310720 | tf_op jit(solution)/shard_map/all_to_all | solution.py:261
  581.8 19.4 %all_to_all.62 = bf16[256,8,4,40]{0,3,1,2:T(8,128)(2,1)S(1)} all-to-all(bf16[256,8,4,40]{0,3,1,2:T(8,128)(2,1)S(1)} %copy.68), channel_id=1, replica_groups=mesh['dp'=8,'seq'=4] {'seq'}, dimensions={2} | all-to-all | bytes 1310720 | tf_op jit(solution)/shard_map/all_to_all | solution.py:268
  606.0 17.5 %all_to_all.63 = bf16[256,8,4,40]{0,3,1,2:T(8,128)(2,1)S(1)} all-to-all(bf16[256,8,4,40]{0,3,1,2:T(8,128)(2,1)S(1)} %copy.71), channel_id=1, replica_groups=mesh['dp'=8,'seq'=4] {'seq'}, dimensions={2} | all-to-all | bytes 1310720 | tf_op jit(solution)/shard_map/all_to_all | solution.py:275
  644.7 49.2 %reduce-scatter.17.cloned.1.call-done = bf16[40,1280]{1,0:T(8,128)(2,1)} async-done(((bf16[320,1280]{1,0:T(8,128)(2,1)}), bf16[40,1280]{1,0:T(8,128)(2,1)}) %reduce-scatter.17.cloned.1.call-update) | async-done | bytes 102416 | tf_op jit(solution)/shard_map/reduce_scatter | solution.py:325
  695.5 24.9 %all-gather.39.cloned.1.call-done = bf16[1024,1280]{0,1:T(8,128)(2,1)} async-done(((bf16[256,1280]{0,1:T(8,128)(2,1)}), bf16[1024,1280]{0,1:T(8,128)(2,1)}) %all-gather.39.cloned.1.call-update) | async-done | bytes 2621456 | tf_op jit(solution)/shard_map/all_gather | solution.py:297
  730.4 39.9 %all-reduce.10 = (f32[1280]{0:T(1024)S(1)}, f32[1280]{0:T(1024)S(1)}, f32[1280]{0:T(1024)S(1)}, f32[1280]{0:T(1024)S(1)}, f32[1280]{0:T(1024)S(1)}) all-reduce(f32[1280]{0:T(1024)S(1)} %get-tuple-element.73, f32[1280]{0:T(1024)S(1)} %reduce_sum.113, f32[1280]{0:T(1024)S(1)} %fusion.28, ...), channel_id=8, replica_groups=mesh['dp'=8,'seq'=4] {'dp','seq'}, use_global_device_ids=true, to_apply=%region_8.9.clone | all-reduce | flops 6400 | bytes 51200
  782.8 58.1 %reduce-scatter.13.cloned.1.call-done = bf16[40,1280]{1,0:T(8,128)(2,1)} async-done(((bf16[320,1280]{1,0:T(8,128)(2,1)}), bf16[40,1280]{1,0:T(8,128)(2,1)}) %reduce-scatter.13.cloned.1.call-update) | async-done | bytes 102416 | tf_op jit(solution)/shard_map/reduce_scatter | solution.py:319
  842.5 58.3 %reduce-scatter.15.cloned.1.call-done = bf16[40,1280]{1,0:T(8,128)(2,1)} async-done(((bf16[320,1280]{1,0:T(8,128)(2,1)}), bf16[40,1280]{1,0:T(8,128)(2,1)}) %reduce-scatter.15.cloned.1.call-update) | async-done | bytes 102416 | tf_op jit(solution)/shard_map/reduce_scatter | solution.py:322
  902.4 58.1 %reduce-scatter.9.cloned.1.call-done = bf16[40,1280]{1,0:T(8,128)(2,1)} async-done(((bf16[320,1280]{1,0:T(8,128)(2,1)}), bf16[40,1280]{1,0:T(8,128)(2,1)}) %reduce-scatter.9.cloned.1.call-update) | async-done | bytes 102416 | tf_op jit(solution)/shard_map/reduce_scatter | solution.py:313
  962.1 58.4 %reduce-scatter.11.cloned.1.call-done = bf16[40,1280]{1,0:T(8,128)(2,1)} async-done(((bf16[320,1280]{1,0:T(8,128)(2,1)}), bf16[40,1280]{1,0:T(8,128)(2,1)}) %reduce-scatter.11.cloned.1.call-update) | async-done | bytes 102416 | tf_op jit(solution)/shard_map/reduce_scatter | solution.py:316
  (243 shorter events, 195.4 us)
Async XLA Ops:
  7.2 65.9 %all-gather.27.cloned.1.call-start = ((), (), s32[]{:S(2)}) async-start(), calls=%async_computation.12 | async-start | bytes 3379200 | tf_op jit(solution)/shard_map/all_gather | solution.py:64
  7.9 126.2 %all-gather.23.cloned.1.call-start = ((), (), s32[]{:S(2)}) async-start(), calls=%async_computation.10 | async-start | bytes 3379200 | tf_op jit(solution)/shard_map/all_gather | solution.py:65
  8.7 186.6 %all-gather.25.cloned.1.call-start = ((), (), s32[]{:S(2)}) async-start(), calls=%async_computation.11 | async-start | bytes 3379200 | tf_op jit(solution)/shard_map/all_gather | solution.py:61
  9.4 211.7 %all-gather.49.cloned.1.call-start = ((), (), s32[]{:S(2)}) async-start(), calls=%async_computation.29 | async-start | bytes 3276800 | tf_op jit(solution)/shard_map/all_gather | solution.py:111
  56.2 139.0 %copy-start.27 = (f32[1280]{0:T(1024)}, f32[1280]{0:T(1024)S(1)}, u32[]{:S(2)}) copy-start(f32[1280]{0:T(1024)S(1)} %convert_element_type.170) | copy-start | bytes 15364
  57.5 137.7 %copy-start.37 = (f32[256]{0:T(256)}, f32[256]{0:T(256)S(1)}, u32[]{:S(2)}) copy-start(f32[256]{0:T(256)S(1)} %add_rsqrt_fusion.1) | copy-start | bytes 3076
  77.1 171.6 %all-gather.47.cloned.1.call-start = ((), (), s32[]{:S(2)}) async-start(), calls=%async_computation.28 | async-start | bytes 3276800 | tf_op jit(solution)/shard_map/all_gather | solution.py:112
  138.0 172.8 %all-gather.29.cloned.1.call-start = ((), (), s32[]{:S(2)}) async-start(), calls=%async_computation.13 | async-start | bytes 3379200 | tf_op jit(solution)/shard_map/all_gather | solution.py:67
  138.6 233.3 %all-gather.31.cloned.1.call-start = ((), (), s32[]{:S(2)}) async-start(), calls=%async_computation.14 | async-start | bytes 3379200 | tf_op jit(solution)/shard_map/all_gather | solution.py:69
  139.3 293.6 %all-gather.33.cloned.1.call-start = ((), (), s32[]{:S(2)}) async-start(), calls=%async_computation.15 | async-start | bytes 3379200 | tf_op jit(solution)/shard_map/all_gather | solution.py:70
  140.1 351.3 %all-gather.51.cloned.1.call-start = ((), (), s32[]{:S(2)}) async-start(), calls=%async_computation.30 | async-start | bytes 3276800 | tf_op jit(solution)/shard_map/all_gather | solution.py:205
  200.4 316.6 %all-gather.53.cloned.1.call-start = ((), (), s32[]{:S(2)}) async-start(), calls=%async_computation.31 | async-start | bytes 3276800 | tf_op jit(solution)/shard_map/all_gather | solution.py:206
  448.5 101.0 %all-gather.45.cloned.1.call-start = ((), (), s32[]{:S(2)}) async-start(), calls=%async_computation.26 | async-start | bytes 3276800 | tf_op jit(solution)/shard_map/all_gather | solution.py:300
  449.2 128.3 %all-gather.35.cloned.1.call-start = ((), (), s32[]{:S(2)}) async-start(), calls=%async_computation.16 | async-start | bytes 3276800 | tf_op jit(solution)/shard_map/all_gather | solution.py:295
  487.0 114.9 %all-gather.41.cloned.1.call-start = ((), (), s32[]{:S(2)}) async-start(), calls=%async_computation.22 | async-start | bytes 3276800 | tf_op jit(solution)/shard_map/all_gather | solution.py:298
  487.7 136.4 %all-gather.43.cloned.1.call-start = ((), (), s32[]{:S(2)}) async-start(), calls=%async_computation.24 | async-start | bytes 3276800 | tf_op jit(solution)/shard_map/all_gather | solution.py:299
  488.3 146.2 %all-gather.37.cloned.1.call-start = ((), (), s32[]{:S(2)}) async-start(), calls=%async_computation.18 | async-start | bytes 3276800 | tf_op jit(solution)/shard_map/all_gather | solution.py:296
  533.9 160.0 %reduce-scatter.17.cloned.1.call-start = ((), (), s32[]{:S(2)}) async-start(), calls=%async_computation.27 | async-start | bytes 921600 | tf_op jit(solution)/shard_map/reduce_scatter | solution.py:325
  553.8 166.6 %all-gather.39.cloned.1.call-start = ((), (), s32[]{:S(2)}) async-start(), calls=%async_computation.20 | async-start | bytes 3276800 | tf_op jit(solution)/shard_map/all_gather | solution.py:297
  563.1 218.1 %reduce-scatter.7.cloned.1.call-start = ((), (), s32[]{:S(2)}) async-start(), calls=%async_computation.17 | async-start | bytes 921600 | tf_op jit(solution)/shard_map/reduce_scatter | solution.py:310
  581.7 259.2 %reduce-scatter.13.cloned.1.call-start = ((), (), s32[]{:S(2)}) async-start(), calls=%async_computation.23 | async-start | bytes 921600 | tf_op jit(solution)/shard_map/reduce_scatter | solution.py:319
  605.6 295.2 %reduce-scatter.15.cloned.1.call-start = ((), (), s32[]{:S(2)}) async-start(), calls=%async_computation.25 | async-start | bytes 921600 | tf_op jit(solution)/shard_map/reduce_scatter | solution.py:322
  627.9 332.6 %reduce-scatter.9.cloned.1.call-start = ((), (), s32[]{:S(2)}) async-start(), calls=%async_computation.19 | async-start | bytes 921600 | tf_op jit(solution)/shard_map/reduce_scatter | solution.py:313
  638.4 382.1 %reduce-scatter.11.cloned.1.call-start = ((), (), s32[]{:S(2)}) async-start(), calls=%async_computation.21 | async-start | bytes 921600 | tf_op jit(solution)/shard_map/reduce_scatter | solution.py:316
  (46 other events, 935.8 us)
Sparse Core Ops, SparseCore 0:
  10.9 62.1 all-gather.26
  75.9 58.1 all-gather.22
  137.0 58.1 all-gather.24
  196.6 24.4 all-gather.48
  223.1 25.5 all-gather.46
  251.4 59.3 all-gather.28
  313.6 58.1 all-gather.30
  374.7 58.1 all-gather.32
  434.5 24.4 all-gather.50
  460.4 25.5 all-gather.52
  487.5 26.2 all-gather.44
  515.2 25.5 all-gather.34
  542.4 26.3 all-gather.40
  570.2 32.0 all-gather.42
  603.7 30.8 all-gather.36
  637.7 56.0 reduce-scatter.16
  695.3 24.9 all-gather.38
  723.9 57.2 reduce-scatter.6
  784.6 56.3 reduce-scatter.12
  844.5 56.2 reduce-scatter.14
  904.1 56.2 reduce-scatter.8
  964.2 56.2 reduce-scatter.10
where the time goes:
time: 1040 us; the launch traced here: 1030 us
  waiting for transfers between devices  639 us (61%)
  blocking collectives  158 us (15%)
  matrix products  142 us (14%)
  local copies, waits for them, and re-layouts  44.7 us (4%)
  other arithmetic  27.9 us (3%)
  between operations  16.2 us (2%)
    unnamed x2, blocking collectives  82.4 us
    reduce_scatter x1, waiting for transfers between devices, shards(): lax.psum_scatter(part_value_mat.astype(jnp.bfloat16), 'dp', scatter_dimen...  58.4 us
    reduce_scatter x1, waiting for transfers between devices, shards(): lax.psum_scatter(part_hidden_mat.astype(jnp.bfloat16), 'dp', scatter_dime...  58.3 us
    reduce_scatter x1, waiting for transfers between devices, shards(): lax.psum_scatter(part_output_mat.astype(jnp.bfloat16), 'dp', scatter_dime...  58.1 us
    reduce_scatter x1, waiting for transfers between devices, shards(): lax.psum_scatter(part_key_mat.astype(jnp.bfloat16), 'dp', scatter_dimensi...  58.1 us
    all_gather x1, waiting for transfers between devices, shards(): lax.all_gather(w_value, ('dp', 'seq'), axis=0, tiled=True)  56.9 us
    all_gather x1, waiting for transfers between devices, shards(): lax.all_gather(w_back, ('dp', 'seq'), axis=0, tiled=True)  56.6 us
    all_gather x1, waiting for transfers between devices, shards(): lax.all_gather(w_hidden, ('dp', 'seq'), axis=0, tiled=True)  55.7 us
  transfers between devices with their start and end apart: 22, of which 16 were waited for; matrix products, arithmetic and copies ran while one was open for 20% of the time, Pallas kernels for 0%

commit v1 on v0

--- a/solution.py
+++ b/solution.py
@@ -3,6 +3,8 @@
 import jax
 import jax.numpy as jnp
 from jax import lax
+from jax.experimental import pallas as pl
+from jax.experimental.pallas import tpu as pltpu
 from jax.sharding import PartitionSpec as P
 
 HEADS = 16
@@ -350,6 +352,868 @@
     )
 
 
+F32 = jnp.float32
+BF16 = jnp.bfloat16
+MESH_ID = pl.DeviceIdType.MESH
+ROWS = 256
+WIDTH = 1280
+SHARE = 40
+MINE = 320
+GROUP_HEADS = 4
+SLOTS = 1024
+PACK = 1024
+
+
+def fits(mesh):
+    return mesh.shape["dp"] == 8 and mesh.shape["seq"] == 4
+
+
+def dot_nn(left, right):
+    return jnp.dot(left, right, preferred_element_type=F32)
+
+
+def dot_nt(left, right):
+    return lax.dot_general(left, right, (((1,), (1,)), ((), ())), preferred_element_type=F32)
+
+
+def dot_tn(left, right):
+    return lax.dot_general(left, right, (((0,), (0,)), ((), ())), preferred_element_type=F32)
+
+
+def tile(index, size):
+    return pl.ds(pl.multiple_of(index * size, size), size)
+
+
+def strip(xx, yy):
+    return pl.ds(pl.multiple_of((xx * 2 + yy) * 2 * SHARE, 16), 2 * SHARE)
+
+
+def half(cc):
+    return pl.ds(pl.multiple_of(cc * (WIDTH // 2), 128), WIDTH // 2)
+
+
+class Links:
+    def __init__(self, send_sems, recv_sems):
+        self.send_sems, self.recv_sems = send_sems, recv_sems
+        self.count = 0
+        self.open = {}
+
+    def send(self, key, src, dst, device):
+        index = self.count
+        self.count += 1
+        copy = pltpu.make_async_remote_copy(
+            src_ref=src,
+            dst_ref=dst,
+            send_sem=self.send_sems.at[index],
+            recv_sem=self.recv_sems.at[index],
+            device_id=device,
+            device_id_type=MESH_ID,
+        )
+        copy.start()
+        self.open[key] = copy
+
+    def recv(self, *keys):
+        for key in keys:
+            self.open[key].wait_recv()
+
+    def sent(self, *keys):
+        for key in keys:
+            self.open.pop(key).wait_send()
+
+    def sent_all(self):
+        for key in list(self.open):
+            self.open.pop(key).wait_send()
+
+
+def layer_kernel(
+    x_ref,
+    len_ref,
+    cot_ref,
+    vec_ref,
+    wq_ref,
+    wk_ref,
+    wv_ref,
+    wo_ref,
+    wh_ref,
+    wb_ref,
+    out_ref,
+    ig_ref,
+    gvec_ref,
+    gq_ref,
+    gk_ref,
+    gv_ref,
+    go_ref,
+    gh_ref,
+    gb_ref,
+    full_o,
+    full_h,
+    full_b,
+    part_b,
+    core_in,
+    far_in,
+    near_in,
+    last_in,
+    qkv_w,
+    stage,
+    tokens,
+    keys,
+    vals,
+    queries_t,
+    keys_t,
+    vals_t,
+    queries_n,
+    lse,
+    mix_out,
+    mix_in,
+    mix,
+    middle,
+    hidden,
+    norm2,
+    active,
+    gmix_out,
+    gmix_in,
+    grad_low,
+    dk_acc,
+    dv_acc,
+    dq_t,
+    grads,
+    unit_core,
+    unit_far,
+    qkv_part,
+    qkv_near,
+    qkv_last,
+    qkv_home,
+    qkv_sum,
+    vec_slots,
+    vec_row,
+    vec_part,
+    vec_in,
+    qkv_own,
+    pair_in,
+    give_out,
+    give_in,
+    mix_send,
+    mix_recv,
+    send_sems,
+    recv_sems,
+):
+    d = lax.axis_index("dp")
+    s = lax.axis_index("seq")
+    z, x = d // 2, d % 2
+    y, c = s // 2, s % 2
+    links = Links(send_sems, recv_sems)
+    send, recv = links.send, links.recv
+    core_dev = (d, y * 2 + (1 - c))
+    y_dev = (d, (1 - y) * 2 + c)
+    yc_dev = (d, (1 - y) * 2 + (1 - c))
+    x_dev = (z * 2 + (1 - x), s)
+    zs = [None] + [(z + k) % 4 for k in range(1, 4)]
+    from_z = [None] + [(z + 4 - k) % 4 for k in range(1, 4)]
+    z_devs = [None] + [(zs[k] * 2 + x, s) for k in range(1, 4)]
+
+    barrier = pltpu.get_barrier_semaphore()
+    for device in (core_dev, y_dev, yc_dev, x_dev, z_devs[1], z_devs[2], z_devs[3]):
+        pl.semaphore_signal(barrier, inc=1, device_id=device, device_id_type=MESH_ID)
+
+    for member in range(4):
+        cols = slice(MINE * member, MINE * (member + 1))
+        stage[member] = jnp.concatenate(
+            [wq_ref[:, cols], wk_ref[:, cols], wv_ref[:, cols], jnp.zeros((SHARE, 64), BF16)], axis=1
+        )
+    qkv_own[s] = stage[s]
+    tokens[s] = x_ref[...]
+    vec_slots[z, x, y, c] = vec_ref[...]
+    shards = {"o": wo_ref, "h": wh_ref, "b": wb_ref}
+    slot_of = {"o": 0, "h": 1, "b": 2}
+    for m in "ohb":
+        pair_in[slot_of[m], c] = shards[m][:, half(c)]
+    pl.semaphore_wait(barrier, 7)
+
+    group = ((1, core_dev), (2, y_dev), (3, yc_dev))
+    peers = (None, y * 2 + (1 - c), (1 - y) * 2 + c, (1 - y) * 2 + (1 - c))
+    for k, device in ((2, y_dev), (3, yc_dev), (1, core_dev)):
+        send(("a2a", k), stage.at[peers[k]], qkv_own.at[s], device)
+    for m in "ohb":
+        send(("pair", m), shards[m].at[:, half(1 - c)], pair_in.at[slot_of[m], c], core_dev)
+    for k in (1, 2, 3):
+        send(("vz", k), vec_ref, vec_slots.at[z, x, y, c], z_devs[k])
+    send("xy", x_ref, tokens.at[s], y_dev)
+    send("xc", x_ref, tokens.at[s], core_dev)
+
+    fulls = {"o": full_o, "h": full_h, "b": full_b}
+    near_axis = {"o": "x", "h": "x", "b": "y"}
+
+    def strip_of(axis, near, far):
+        if axis == "x":
+            return strip(x if near == 0 else 1 - x, y if far == 0 else 1 - y)
+        return strip(x if far == 0 else 1 - x, y if near == 0 else 1 - y)
+
+    def devs(m):
+        return (x_dev, y_dev) if near_axis[m] == "x" else (y_dev, x_dev)
+
+    def gather_z(m):
+        for k in (1, 2, 3):
+            piece = fulls[m].at[z, strip(x, y), half(c)]
+            send((m, "z", k), piece, piece, z_devs[k])
+
+    def gather_own(m):
+        near_dev, far_dev = devs(m)
+        piece = fulls[m].at[z, strip(x, y), half(c)]
+        send((m, "n", 0), piece, piece, near_dev)
+        send((m, "f", 0), piece, piece, far_dev)
+
+    def gather_near(m, k):
+        near_dev, far_dev = devs(m)
+        recv((m, "z", k))
+        piece = fulls[m].at[from_z[k], strip(x, y), half(c)]
+        send((m, "n", k), piece, piece, near_dev)
+        send((m, "f", k), piece, piece, far_dev)
+
+    def all_z(m, near, far):
+        return fulls[m].at[:, strip_of(near_axis[m], near, far), half(c)]
+
+    def gather_far(m):
+        near_dev, far_dev = devs(m)
+        piece = all_z(m, 0, 0)
+        send((m, "c", 0), piece, piece, core_dev)
+        recv(*[(m, "n", k) for k in range(4)])
+        piece = all_z(m, 1, 0)
+        send((m, "f", 4), piece, piece, far_dev)
+        send((m, "c", 1), piece, piece, core_dev)
+
+    def gather_core(m, part):
+        if part == 0:
+            recv(*[(m, "f", k) for k in range(4)])
+            piece = all_z(m, 0, 1)
+            send((m, "c", 2), piece, piece, core_dev)
+        else:
+            recv((m, "f", 4))
+            piece = all_z(m, 1, 1)
+            send((m, "c", 3), piece, piece, core_dev)
+
+    def gather_done(m):
+        recv(*[(m, "c", k) for k in range(4)])
+
+    for m in "ohb":
+        recv(("pair", m))
+        fulls[m][z, strip(x, y), half(c)] = jnp.concatenate(
+            [pair_in[slot_of[m], 0], pair_in[slot_of[m], 1]], axis=0
+        )
+    gather_z("o")
+    gather_own("o")
+    gather_own("h")
+    gather_own("b")
+    recv(("a2a", 1), ("a2a", 2), ("a2a", 3))
+    qkv_w[d] = jnp.concatenate([qkv_own[member] for member in range(4)], axis=0)
+    for k in (1, 2, 3):
+        send(("wz", k), qkv_w.at[d], qkv_w.at[d], z_devs[k])
+    send(("wx", 0), qkv_w.at[d], qkv_w.at[d], x_dev)
+    gather_z("h")
+    gather_z("b")
+    recv(("vz", 1), ("vz", 2), ("vz", 3))
+    piece = vec_slots.at[:, x, y, c]
+    send("vx", piece, piece, x_dev)
+    gather_near("o", 1)
+    gather_near("o", 2)
+    gather_near("o", 3)
+    recv("vx")
+    piece = vec_slots.at[:, :, y, c]
+    send("vy", piece, piece, y_dev)
+    recv("xy")
+    piece = tokens.at[peers[2]]
+    send("xyc", piece, piece, core_dev)
+    recv("vy")
+    piece = vec_slots.at[:, :, :, c]
+    send("vc", piece, piece, core_dev)
+
+    def qkv_near_step(k):
+        recv(("wz", k))
+        row = from_z[k] * 2 + x
+        send(("wx", k), qkv_w.at[row], qkv_w.at[row], x_dev)
+
+    gather_far("o")
+    qkv_near_step(1)
+    recv("vc")
+    vec_row[...] = jnp.zeros_like(vec_row)
+    for slot in range(32):
+        start = slot * SHARE
+        low = start // 128 * 128
+        piece = jnp.concatenate(
+            [vec_slots[slot // 8, slot // 4 % 2, slot // 2 % 2, slot % 2], jnp.zeros((8, 128), F32)], axis=1
+        )
+        if start > low:
+            piece = pltpu.roll(piece, start - low, 1)
+        vec_row[:, low : low + 256] += piece
+    recv("xc", "xyc")
+    links.sent("xyc")
+
+    def norm_rows(step, carry):
+        for member in range(4):
+            rows = tile(step, 64)
+            value = tokens[member, rows, :].astype(F32)
+            unit = value * lax.rsqrt(jnp.mean(value * value, axis=-1, keepdims=True) + 1e-06)
+            tokens[member, rows, :] = (unit * vec_row[0:1, :WIDTH]).astype(BF16)
+        return carry
+
+    lax.fori_loop(0, ROWS // 64, norm_rows, 0)
+    qkv_near_step(2)
+    gather_core("o", 0)
+    gather_core("o", 1)
+    qkv_near_step(3)
+
+    def own(row):
+        value = vec_row[row : row + 1, 0:MINE]
+        for member in range(1, 4):
+            value = jnp.where(s == member, vec_row[row : row + 1, MINE * member : MINE * (member + 1)], value)
+        return value
+
+    query_log = own(2)
+    factor = query_gain / math.sqrt(HEAD_DIM)
+    scale = (jnp.maximum(query_log, 0.0) + jnp.log1p(jnp.exp(-jnp.abs(query_log)))) * factor
+    query_bias, value_bias = own(1), own(3)
+
+    recv(*[("wx", k) for k in range(4)])
+    weights = qkv_w.reshape(WIDTH, PACK)
+
+    def project(i, carry):
+        rows = tile(i, ROWS)
+        raw = dot_nn(tokens[i], weights[...])
+        query = ((raw[:, :MINE] + query_bias) * scale).astype(BF16)
+        key = raw[:, MINE : 2 * MINE].astype(BF16)
+        val = (raw[:, 2 * MINE : 3 * MINE] + value_bias).astype(BF16)
+        queries_n[i] = query
+        queries_t[:, rows] = query.T
+        keys_t[:, rows] = key.T
+        vals_t[:, rows] = val.T
+        for h in range(GROUP_HEADS):
+            keys[h, rows, :] = key[:, HEAD_DIM * h : HEAD_DIM * (h + 1)]
+            vals[h, rows, :] = val[:, HEAD_DIM * h : HEAD_DIM * (h + 1)]
+        return carry
+
+    lax.fori_loop(0, 4, project, 0)
+    for k in (1, 2, 3):
+        gather_near("h", k)
+
+    key_place = lax.broadcasted_iota(jnp.int32, (ROWS, ROWS), 0)
+    query_place = lax.broadcasted_iota(jnp.int32, (ROWS, ROWS), 1)
+    allowed = key_place <= query_place
+
+    def attend(i):
+        low, high = i * ROWS, (i + 1) * ROWS
+
+        def head(h, carry):
+            rows = tile(h, HEAD_DIM)
+            query = queries_t[rows, low:high]
+            near = jnp.where(allowed, dot_nn(keys[h, low:high, :], query), masked_score)
+            largest = jnp.max(near, axis=0, keepdims=True)
+            if i:
+                before = dot_nn(keys[h, 0:low, :], query)
+                largest = jnp.maximum(largest, jnp.max(before, axis=0, keepdims=True))
+            near = jnp.exp(near - largest)
+            total = jnp.sum(near, axis=0, keepdims=True)
+            mixed = dot_nn(vals_t[rows, low:high], near.astype(BF16))
+            if i:
+                before = jnp.exp(before - largest)
+                total += jnp.sum(before, axis=0, keepdims=True)
+                mixed += dot_nn(vals_t[rows, 0:low], before.astype(BF16))
+            lse[h, :, low:high] = largest + jnp.log(total)
+            mix_out[i, rows, :] = (mixed / total).astype(BF16)
+            return carry
+
+        lax.fori_loop(0, GROUP_HEADS, head, 0)
+
+    def mix_copy(dest, source):
+        return pltpu.make_async_remote_copy(
+            src_ref=mix_out.at[dest],
+            dst_ref=mix_in.at[source],
+            send_sem=mix_send.at[dest],
+            recv_sem=mix_recv.at[source],
+            device_id=(d, dest),
+            device_id_type=MESH_ID,
+        )
+
+    for i in (3, 2, 1, 0):
+        attend(i)
+
+        @pl.when(s != i)
+        def _():
+            mix_copy(i, s).start()
+
+        @pl.when(s == i)
+        def _():
+            mix_in[i] = mix_out[i]
+
+        if i == 3:
+            gather_far("h")
+        if i == 2:
+            gather_near("b", 1)
+            gather_near("b", 2)
+        if i == 1:
+            gather_near("b", 3)
+
+    gather_done("o")
+    for k in (1, 2, 3):
+        mix_copy(peers[k], peers[k]).wait_recv()
+
+    mix[...] = mix_in[...].reshape(WIDTH, ROWS).T
+    mats = {m: fulls[m].reshape(WIDTH, WIDTH) for m in "ohb"}
+
+    def middle_step(j, carry):
+        cols = tile(j, 256)
+        middle[:, cols] = x_ref[:, cols].astype(F32) + dot_nn(mix[...], mats["o"][:, cols])
+        return carry
+
+    lax.fori_loop(0, 5, middle_step, 0)
+
+    def rms_inverse(value):
+        return lax.rsqrt(jnp.mean(value * value, axis=-1, keepdims=True) + 1e-06)
+
+    def norm_two(step, carry):
+        rows = tile(step, 64)
+        value = middle[rows, :]
+        norm2[rows, :] = (value * rms_inverse(value) * vec_row[4:5, :WIDTH]).astype(BF16)
+        return carry
+
+    lax.fori_loop(0, ROWS // 64, norm_two, 0)
+    gather_far("b")
+    gather_core("h", 0)
+    gather_core("h", 1)
+    gather_done("h")
+
+    def hidden_step(j, carry):
+        cols = tile(j, 256)
+        value = dot_nn(norm2[...], mats["h"][:, cols])
+        hidden[:, cols] = value
+        active[:, cols] = (value * jax.nn.sigmoid(value)).astype(BF16)
+        return carry
+
+    lax.fori_loop(0, 5, hidden_step, 0)
+
+    place = s * ROWS + lax.broadcasted_iota(jnp.int32, (ROWS, 1), 0)
+    valid = place < len_ref[0]
+
+    def grad_y():
+        return jnp.where(valid, cot_ref[...], jnp.zeros((ROWS, WIDTH), BF16))
+
+    parts = {"b": part_b, "h": full_b, "o": full_h}
+    far_axis = {"b": "x", "h": "x", "o": "y"}
+    outs = {"b": gb_ref, "h": gh_ref, "o": go_ref}
+    order = {"b": 0, "h": 1, "o": 2}
+
+    def weight_grad(m, left):
+        flat = parts[m].reshape(WIDTH, WIDTH)
+        right = grad_y() if m == "b" else grad_low[...]
+
+        def step(j, carry):
+            flat[tile(j, 256), :] = left(j, right).astype(BF16)
+            return carry
+
+        lax.fori_loop(0, 5, step, 0)
+
+    def part_at(m, far, near, cc):
+        return parts[m].at[:, strip_of(far_axis[m], far, near), half(cc)]
+
+    def core_at(m, far, near):
+        ref = core_in.at[order[m]]
+        if far_axis[m] == "x":
+            return ref.at[:, x if far == 0 else 1 - x, y if near == 0 else 1 - y]
+        return ref.at[:, x if near == 0 else 1 - x, y if far == 0 else 1 - y]
+
+    def add_into(target, other):
+        def step(zz, carry):
+            target[zz] = (target[zz].astype(F32) + other[zz].astype(F32)).astype(BF16)
+            return carry
+
+        lax.fori_loop(0, 4, step, 0)
+
+    def grad_devs(m):
+        return (x_dev, y_dev) if far_axis[m] == "x" else (y_dev, x_dev)
+
+    def scatter_core(m):
+        for far in (1, 0):
+            for near in (1, 0):
+                send((m, "gc", far, near), part_at(m, far, near, 1 - c), core_at(m, far, near), core_dev)
+
+    def scatter_far(m):
+        far_dev, near_dev = grad_devs(m)
+        for near in (1, 0):
+            recv((m, "gc", 1, near))
+            add_into(part_at(m, 1, near, c), core_at(m, 1, near))
+            send((m, "gf", near), part_at(m, 1, near, c), far_in.at[order[m], near], far_dev)
+        for near in (1, 0):
+            recv((m, "gc", 0, near))
+            add_into(part_at(m, 0, near, c), core_at(m, 0, near))
+
+    def scatter_near(m):
+        far_dev, near_dev = grad_devs(m)
+        recv((m, "gf", 1))
+        add_into(part_at(m, 0, 1, c), far_in.at[order[m], 1])
+        send((m, "gn"), part_at(m, 0, 1, c), near_in.at[order[m]], near_dev)
+        recv((m, "gf", 0))
+        add_into(part_at(m, 0, 0, c), far_in.at[order[m], 0])
+
+    def scatter_z(m):
+        recv((m, "gn"))
+        add_into(part_at(m, 0, 0, c), near_in.at[order[m]])
+        for k in (1, 2, 3):
+            send((m, "gz", k), part_at(m, 0, 0, c).at[zs[k]], last_in.at[order[m], k - 1], z_devs[k])
+
+    def scatter_sum(m):
+        total = part_at(m, 0, 0, c)[z].astype(F32)
+        for k in (1, 2, 3):
+            recv((m, "gz", k))
+            total += last_in[order[m], k - 1].astype(F32)
+        outs[m][:, half(c)] = jnp.where(c == 0, total[:SHARE], total[SHARE:])
+        give_out[order[m]] = jnp.where(c == 0, total[SHARE:], total[:SHARE])
+        send((m, "give"), give_out.at[order[m]], give_in.at[order[m]], core_dev)
+
+    def scatter_done(m):
+        recv((m, "give"))
+        outs[m][:, half(1 - c)] = give_in[order[m]]
+
+    weight_grad("b", lambda j, right: dot_tn(active[:, tile(j, 256)], right))
+    scatter_core("b")
+    gather_core("b", 0)
+    gather_core("b", 1)
+    gather_done("b")
+    scatter_far("b")
+
+    def back_step(j, carry):
+        cols = tile(j, 256)
+        value = hidden[:, cols]
+        sigma = jax.nn.sigmoid(value)
+        grad = dot_nt(grad_y(), mats["b"][cols, :])
+        grad_low[:, cols] = (grad * sigma * (1.0 + value * (1.0 - sigma))).astype(BF16)
+        out_ref[:, cols] = jnp.where(
+            valid, middle[:, cols] + dot_nn(active[...], mats["b"][:, cols]), 0.0
+        ).astype(BF16)
+        return carry
+
+    lax.fori_loop(0, 5, back_step, 0)
+    links.sent(*[("b", "c", k) for k in range(4)], *[("b", "z", k) for k in (1, 2, 3)])
+    links.sent(*[("b", kind, k) for kind in "nf" for k in range(4)], ("b", "f", 4))
+    weight_grad("h", lambda j, right: dot_tn(norm2[:, tile(j, 256)], right))
+    scatter_core("h")
+
+    def normed_step(j, carry):
+        hidden[:, tile(j, 256)] = dot_nt(grad_low[...], mats["h"][tile(j, 256), :])
+        return carry
+
+    lax.fori_loop(0, 5, normed_step, 0)
+    vec_part[...] = jnp.zeros_like(vec_part)
+
+    def middle_back(step, carry):
+        rows = tile(step, 64)
+        value = middle[rows, :]
+        inverse = rms_inverse(value)
+        unit = value * inverse
+        grad = hidden[rows, :]
+        vec_part[4:5, :] += jnp.sum(grad * unit, axis=0, keepdims=True)
+        scaled = grad * vec_row[4:5, :WIDTH]
+        inside = (s * ROWS + step * 64 + lax.broadcasted_iota(jnp.int32, (64, 1), 0)) < len_ref[0]
+        base = jnp.where(inside, cot_ref[rows, :].astype(F32), 0.0)
+        total = base + inverse * (scaled - unit * jnp.mean(scaled * unit, axis=-1, keepdims=True))
+        ig_ref[rows, :] = total
+        grad_low[rows, :] = total.astype(BF16)
+        return carry
+
+    lax.fori_loop(0, ROWS // 64, middle_back, 0)
+
+    def mixed_back(member, carry):
+        gmix_out[member] = dot_nt(mats["o"][tile(member, MINE), :], grad_low[...]).astype(BF16)
+        return carry
+
+    lax.fori_loop(0, 4, mixed_back, 0)
+    for k, device in ((2, y_dev), (3, yc_dev), (1, core_dev)):
+        send(("gm", k), gmix_out.at[peers[k]], gmix_in.at[s], device)
+    gmix_in[s] = gmix_out[s]
+    scatter_far("h")
+    links.sent(*[("h", "c", k) for k in range(4)], *[("h", "z", k) for k in (1, 2, 3)])
+    links.sent(*[("h", kind, k) for kind in "nf" for k in range(4)], ("h", "f", 4))
+    mixed_flat = mix_in.reshape(WIDTH, ROWS)
+    weight_grad("o", lambda j, right: dot_nn(mixed_flat[tile(j, 256), :], right))
+    scatter_core("o")
+    scatter_near("b")
+    recv(("gm", 1), ("gm", 2), ("gm", 3))
+    scatter_far("o")
+
+    def attend_back(h):
+        rows = slice(HEAD_DIM * h, HEAD_DIM * (h + 1))
+        dk_acc[...] = jnp.zeros_like(dk_acc)
+        dv_acc[...] = jnp.zeros_like(dv_acc)
+        for i in range(4):
+            low, high = i * ROWS, (i + 1) * ROWS
+            query = queries_t[rows, low:high]
+            grad = gmix_in[i, rows, :]
+            log_total = lse[h, :, low:high]
+            spans = [(0, low), (low, high)] if i else [(low, high)]
+            held = []
+            inner = jnp.zeros((1, ROWS), F32)
+            for first, last in spans:
+                scores = dot_nn(keys[h, first:last, :], query)
+                if first == low:
+                    scores = jnp.where(allowed, scores, masked_score)
+                probs = jnp.exp(scores - log_total)
+                grad_probs = dot_nn(vals[h, first:last, :], grad)
+                inner += jnp.sum(probs * grad_probs, axis=0, keepdims=True)
+                held.append((first, last, probs, grad_probs))
+            grad_query = jnp.zeros((HEAD_DIM, ROWS), F32)
+            for first, last, probs, grad_probs in held:
+                grad_scores = (probs * (grad_probs - inner)).astype(BF16)
+                grad_query += dot_nn(keys_t[rows, first:last], grad_scores)
+                dk_acc[first:last, :] += dot_nt(grad_scores, query)
+                dv_acc[first:last, :] += dot_nt(probs.astype(BF16), grad)
+            dq_t[rows, low:high] = grad_query
+        grads[:, MINE + HEAD_DIM * h : MINE + HEAD_DIM * (h + 1)] = dk_acc[...].astype(BF16)
+        grads[:, 2 * MINE + HEAD_DIM * h : 2 * MINE + HEAD_DIM * (h + 1)] = dv_acc[...].astype(BF16)
+
+    attend_back(0)
+    scatter_near("h")
+    attend_back(1)
+    scatter_z("b")
+    attend_back(2)
+    scatter_near("o")
+    attend_back(3)
+    scatter_z("h")
+    grads[:, 3 * MINE :] = jnp.zeros((SLOTS, PACK - 3 * MINE), BF16)
+    bias_grad = jnp.zeros((1, MINE), F32)
+    scale_grad = jnp.zeros((1, MINE), F32)
+    value_grad = jnp.zeros((1, MINE), F32)
+    for i in range(4):
+        rows = slice(i * ROWS, (i + 1) * ROWS)
+        grad = dq_t[:, rows].T
+        low_grad = (grad * scale).astype(BF16)
+        grads[rows, 0:MINE] = low_grad
+        bias_grad += jnp.sum(low_grad.astype(F32), axis=0, keepdims=True)
+        scale_grad += jnp.sum(grad * queries_n[i].astype(F32), axis=0, keepdims=True)
+        value_grad += jnp.sum(grads[rows, 2 * MINE : 3 * MINE].astype(F32), axis=0, keepdims=True)
+    scale_grad = scale_grad / scale * jax.nn.sigmoid(query_log) * factor
+    for row, value in ((1, bias_grad), (2, scale_grad), (3, value_grad)):
+        vec_part[row : row + 1, :] = jnp.concatenate(
+            [jnp.where(s == member, value, 0.0) for member in range(4)], axis=1
+        )
+
+    flat = qkv_part.reshape(WIDTH, PACK)
+
+    def qkv_grad(j, carry):
+        total = jnp.zeros((256, PACK), F32)
+        for i in range(4):
+            total += dot_tn(tokens[i, :, tile(j, 256)], grads[i * ROWS : (i + 1) * ROWS, :])
+        flat[tile(j, 256), :] = total.astype(BF16)
+        return carry
+
+    lax.fori_loop(0, 5, qkv_grad, 0)
+    for k in (1, 2, 3):
+        send(("px", k), qkv_part.at[zs[k], 1 - x], qkv_near.at[k], x_dev)
+    send(("px", 0), qkv_part.at[z, 1 - x], qkv_near.at[0], x_dev)
+
+    def unit_grad(j, carry):
+        cols = tile(j, 256)
+        for i in range(4):
+            tokens[i, :, cols] = dot_nt(grads[i * ROWS : (i + 1) * ROWS, :], weights[cols, :]).astype(BF16)
+        return carry
+
+    links.sent("xy", "xc")
+    lax.fori_loop(0, 5, unit_grad, 0)
+    for far in (1, 0):
+        member = (y if far == 0 else 1 - y) * 2 + (1 - c)
+        send(("uc", far), tokens.at[member], unit_core.at[far], core_dev)
+    recv(("uc", 1))
+    far_member = (1 - y) * 2 + c
+    tokens[far_member] = (tokens[far_member].astype(F32) + unit_core[1].astype(F32)).astype(BF16)
+    send("uy", tokens.at[far_member], unit_far, y_dev)
+    recv(("uc", 0))
+    scatter_z("o")
+    for k in (1, 2, 3):
+        recv(("px", k))
+        qkv_part[zs[k], x] = (qkv_part[zs[k], x].astype(F32) + qkv_near[k].astype(F32)).astype(BF16)
+        send(("pz", k), qkv_part.at[zs[k], x], qkv_last.at[k - 1], z_devs[k])
+    scatter_sum("b")
+    scatter_sum("h")
+    recv("uy")
+
+    def input_back(step, carry):
+        rows = tile(step, 64)
+        value = x_ref[rows, :].astype(F32)
+        inverse = rms_inverse(value)
+        unit = value * inverse
+        grad = (
+            tokens[s, rows, :].astype(F32) + unit_core[0, rows, :].astype(F32) + unit_far[rows, :].astype(F32)
+        )
+        vec_part[0:1, :] += jnp.sum(grad * unit, axis=0, keepdims=True)
+        scaled = grad * vec_row[0:1, :WIDTH]
+        ig_ref[rows, :] += inverse * (scaled - unit * jnp.mean(scaled * unit, axis=-1, keepdims=True))
+        return carry
+
+    lax.fori_loop(0, ROWS // 64, input_back, 0)
+    send("sc", vec_part, vec_in.at[0], core_dev)
+    recv("sc")
+    links.sent("sc")
+    vec_part[...] += vec_in[0]
+    send("sy", vec_part, vec_in.at[1], y_dev)
+    scatter_sum("o")
+    recv("sy")
+    links.sent("sy")
+    vec_part[...] += vec_in[1]
+    send("sx", vec_part, vec_in.at[2], x_dev)
+    recv("sx")
+    links.sent("sx")
+    vec_part[...] += vec_in[2]
+    for k in (1, 2, 3):
+        send(("sz", k), vec_part, vec_in.at[2 + k], z_devs[k])
+    recv(("px", 0))
+    qkv_part[z, x] = (qkv_part[z, x].astype(F32) + qkv_near[0].astype(F32)).astype(BF16)
+    recv(("pz", 1), ("pz", 2), ("pz", 3))
+    total = qkv_part[z, x].astype(F32)
+    for k in (1, 2, 3):
+        total += qkv_last[k - 1].astype(F32)
+    for member in range(4):
+        qkv_sum[member] = total[SHARE * member : SHARE * (member + 1), :].astype(BF16)
+    for k, device in ((2, y_dev), (3, yc_dev), (1, core_dev)):
+        send(("ph", k), qkv_sum.at[peers[k]], qkv_home.at[s], device)
+    qkv_home[s] = qkv_sum[s]
+    recv(("sz", 1), ("sz", 2), ("sz", 3))
+    total = vec_part[...] + vec_in[3] + vec_in[4] + vec_in[5]
+    gvec_ref[...] = pltpu.roll(total, WIDTH - (d * 4 + s) * SHARE, 1)[:, :128]
+    for m in "bho":
+        scatter_done(m)
+    recv(("ph", 1), ("ph", 2), ("ph", 3))
+    for index, ref in enumerate((gq_ref, gk_ref, gv_ref)):
+        for member in range(4):
+            ref[:, MINE * member : MINE * (member + 1)] = qkv_home[
+                member, :, MINE * index : MINE * (index + 1)
+            ].astype(F32)
+    links.sent_all()
+    for i in range(4):
+
+        @pl.when(s != i)
+        def _():
+            mix_copy(i, s).wait_send()
+
+
+def fused_shards(
+    inputs,
+    lengths,
+    cotangent,
+    gain_attn,
+    w_query,
+    bias_query,
+    query_scale,
+    w_key,
+    w_value,
+    bias_value,
+    w_out,
+    gain_mlp,
+    w_hidden,
+    w_back,
+):
+    rows = jnp.stack([gain_attn, bias_query, query_scale, bias_value, gain_mlp]).astype(F32)
+    vectors = jnp.pad(rows, ((0, 3), (0, 128 - SHARE)))
+    vmem = pl.BlockSpec(memory_space=pltpu.VMEM)
+    whole = (4, 8 * SHARE, WIDTH)
+    buffers = [
+        (whole, BF16),
+        (whole, BF16),
+        (whole, BF16),
+        (whole, BF16),
+        ((3, 4, 2, 2, 2 * SHARE, WIDTH // 2), BF16),
+        ((3, 2, 4, 2 * SHARE, WIDTH // 2), BF16),
+        ((3, 4, 2 * SHARE, WIDTH // 2), BF16),
+        ((3, 3, 2 * SHARE, WIDTH // 2), BF16),
+        ((8, 4 * SHARE, PACK), BF16),
+        ((4, SHARE, PACK), BF16),
+        ((4, ROWS, WIDTH), BF16),
+        ((GROUP_HEADS, SLOTS, HEAD_DIM), BF16),
+        ((GROUP_HEADS, SLOTS, HEAD_DIM), BF16),
+        ((MINE, SLOTS), BF16),
+        ((MINE, SLOTS), BF16),
+        ((MINE, SLOTS), BF16),
+        ((4, ROWS, MINE), BF16),
+        ((GROUP_HEADS, 1, SLOTS), F32),
+        ((4, MINE, ROWS), BF16),
+        ((4, MINE, ROWS), BF16),
+        ((ROWS, WIDTH), BF16),
+        ((ROWS, WIDTH), F32),
+        ((ROWS, WIDTH), F32),
+        ((ROWS, WIDTH), BF16),
+        ((ROWS, WIDTH), BF16),
+        ((4, MINE, ROWS), BF16),
+        ((4, MINE, ROWS), BF16),
+        ((ROWS, WIDTH), BF16),
+        ((SLOTS, HEAD_DIM), F32),
+        ((SLOTS, HEAD_DIM), F32),
+        ((MINE, SLOTS), F32),
+        ((SLOTS, PACK), BF16),
+        ((2, ROWS, WIDTH), BF16),
+        ((ROWS, WIDTH), BF16),
+        ((4, 2, 4 * SHARE, PACK), BF16),
+        ((4, 4 * SHARE, PACK), BF16),
+        ((3, 4 * SHARE, PACK), BF16),
+        ((4, SHARE, PACK), BF16),
+        ((4, SHARE, PACK), BF16),
+        ((4, 2, 2, 2, 8, 128), F32),
+        ((8, WIDTH + 128), F32),
+        ((8, WIDTH), F32),
+        ((6, 8, WIDTH), F32),
+        ((4, SHARE, PACK), BF16),
+        ((3, 2, SHARE, WIDTH // 2), BF16),
+        ((3, SHARE, WIDTH // 2), F32),
+        ((3, SHARE, WIDTH // 2), F32),
+    ]
+    scratch = [pltpu.VMEM(shape, kind) for shape, kind in buffers]
+    scratch += [pltpu.SemaphoreType.DMA((4,)), pltpu.SemaphoreType.DMA((4,))]
+    scratch += [pltpu.SemaphoreType.DMA((128,)), pltpu.SemaphoreType.DMA((128,))]
+    square = jax.ShapeDtypeStruct((SHARE, WIDTH), F32)
+    results = pl.pallas_call(
+        layer_kernel,
+        out_shape=(
+            jax.ShapeDtypeStruct((ROWS, WIDTH), BF16),
+            jax.ShapeDtypeStruct((ROWS, WIDTH), F32),
+            jax.ShapeDtypeStruct((8, 128), F32),
+            square,
+            square,
+            square,
+            square,
+            square,
+            square,
+        ),
+        in_specs=[vmem, pl.BlockSpec(memory_space=pltpu.SMEM)] + [vmem] * 8,
+        out_specs=tuple([vmem] * 9),
+        scratch_shapes=scratch,
+        compiler_params=pltpu.CompilerParams(
+            collective_id=0, has_side_effects=True, vmem_limit_bytes=66 * 1000 * 1000
+        ),
+        cost_estimate=pl.CostEstimate(flops=25_000_000_000, bytes_accessed=10_000_000, transcendentals=10_000_000),
+    )(
+        inputs.reshape(ROWS, WIDTH),
+        lengths,
+        cotangent.reshape(ROWS, WIDTH),
+        vectors,
+        w_query,
+        w_key,
+        w_value,
+        w_out,
+        w_hidden,
+        w_back,
+    )
+    out, input_grad, gvec, gq, gk, gv, go, gh, gb = results
+    return (
+        out.reshape(inputs.shape),
+        input_grad.reshape(inputs.shape),
+        gvec[0, :SHARE],
+        gq,
+        gvec[1, :SHARE],
+        gvec[2, :SHARE],
+        gk,
+        gv,
+        gvec[3, :SHARE],
+        go,
+        gvec[4, :SHARE],
+        gh,
+        gb,
+    )
+
+
 def solution(mesh):
     placed = (
         P("dp", "seq", None),
@@ -368,7 +1232,7 @@
         P(("dp", "seq"), None),
     )
     return jax.shard_map(
-        shards,
+        fused_shards if fits(mesh) else shards,
         mesh=mesh,
         in_specs=placed,
         out_specs=(

time: 1040 us -> 238 us (0.23)
  waiting for transfers between devices: 639 us -> 0 us
  Pallas kernels: 0 us -> 226 us
  blocking collectives: 158 us -> 0 us
  matrix products: 142 us -> 0 us
  local copies, waits for them, and re-layouts: 44.7 us -> 9.27 us
  other arithmetic: 27.9 us -> 0.6 us
  between operations: 16.2 us -> 1.34 us
    all_gather x16 -> x0, waiting for transfers between devices: 347 us -> none  [the longest x1 56.9 us: shards(): lax.all_gather(w_value, ('dp', 'seq'), axis=0, tiled=True)]
    reduce_scatter x6 -> x0, waiting for transfers between devices: 287 us -> none  [the longest x1 58.4 us: shards(): lax.psum_scatter(part_value_mat.astype(jnp.bfloat16), 'dp', scatter_dimen...]
    pallas_call x0 -> x1, Pallas kernels: none -> 226 us  [fused_shards(): pl.pallas_call(layer_kernel, out_shape=(jax.ShapeDtypeStruct((ROWS, WIDTH...]
    dot_general x25 -> x0, matrix products: 142 us -> none  [the longest x6 23.6 us: row_product(): lax.dot_general(left, right, (((0,), (0,)), ((), ())), preferred_element_...]
    unnamed x2 -> x0, blocking collectives: 82.4 us -> none
    all_to_all x4 -> x0, blocking collectives: 62.2 us -> none  [the longest x1 19.4 us: shards(): lax.all_to_all(mixed.reshape(tok_rows, dp_count, seq_count, share), 'seq'...]
    all_gather x4 -> x0, local copies, waits for them, and re-layouts: 14.9 us -> none  [the longest x1 4.48 us: shards(): lax.all_gather(grad_mixed_three, 'seq', axis=1, tiled=True)]
    all_gather x2 -> x0, blocking collectives: 13.3 us -> none  [the longest x1 7.08 us: shards(): lax.all_gather(inner_rows, 'seq', axis=2, tiled=True)]
  transfers between devices with their start and end apart: 22 -> 0, of which waited for: 16 -> 0; matrix products, arithmetic and copies ran while one was open for 20% -> 0% of each run, Pallas kernels for 0% -> 0%
where the time goes in v1:
time: 238 us; the launch traced here: 237 us
  Pallas kernels  226 us (95%)
  local copies, waits for them, and re-layouts  9.27 us (4%)
    pallas_call x1, Pallas kernels, fused_shards(): pl.pallas_call(layer_kernel, out_shape=(jax.ShapeDtypeStruct((ROWS, WIDTH...  226 us
    unnamed x22, local copies, waits for them, and re-layouts  7.13 us

profile of v1, /device:TPU:0, one launch (start us, length us, event | category | flops | bytes accessed | tf_op | source)
XLA Modules:
  0.0 236.8 jit_solution(15008006169876056719)
XLA Ops:
  0.6 0.7 stack.23
  1.4 0.6 pad_convert_fusion.vec_ref
  2.6 225.6 %shard_map.237 = (bf16[256,1280]{1,0:T(8,128)(2,1)}, f32[256,1280]{1,0:T(8,128)}, f32[8,128]{1,0:T(8,128)}, f32[40,1280]{1,0:T(8,128)}, f32[40,1280]{1,0:T(8,128...) custom-call(bf16[256,1280]{1,0:T(8,128)(2,1)} %bitcast.26, ...), custom_call_target="tpu_custom_call" | custom-call | flops 24999999488 | bytes 10000000 | tf_op jit(solution)/shard_map/pallas_call | solution.py:1167
  228.2 0.0 copy-start
  228.2 1.4 slice_bitcast_fusion
  229.6 2.0 copy.36
  231.6 0.0 copy-done
  231.6 0.0 copy-start.6
  231.6 0.0 copy-start.5
  231.6 0.0 copy-start.4
  231.6 0.0 copy-start.3
  231.6 1.1 copy.37
  232.7 0.0 copy-done.6
  232.7 0.7 copy.38
  233.4 0.0 copy-done.5
  233.4 0.7 copy.39
  234.1 0.0 copy-done.4
  234.1 0.7 copy.40
  234.7 0.0 copy-done.3
  234.7 0.7 copy.41
  235.4 0.0 copy-done.2
  235.4 0.7 copy.42
  236.1 0.0 copy-done.1
  236.1 0.7 copy.43
  (2 shorter events, 0.0 us)
Async XLA Ops:
  228.2 3.4 %copy-start = (f32[256,1280]{1,0:T(8,128)S(1)}, f32[256,1280]{1,0:T(8,128)}, u32[]{:S(2)}) copy-start(f32[256,1280]{1,0:T(8,128)} %get-tuple-element.23) | copy-start | bytes 3932164
  231.6 1.1 copy-start.6
  231.6 1.8 copy-start.5
  231.6 2.4 %copy-start.4 = (f32[40,1280]{1,0:T(8,128)S(1)}, f32[40,1280]{1,0:T(8,128)}, u32[]{:S(2)}) copy-start(f32[40,1280]{1,0:T(8,128)} %get-tuple-element.56) | copy-start | bytes 614404
  231.6 3.1 %copy-start.3 = (f32[40,1280]{1,0:T(8,128)S(1)}, f32[40,1280]{1,0:T(8,128)}, u32[]{:S(2)}) copy-start(f32[40,1280]{1,0:T(8,128)} %get-tuple-element.58) | copy-start | bytes 614404
  232.7 2.7 %copy-start.2 = (f32[40,1280]{1,0:T(8,128)S(1)}, f32[40,1280]{1,0:T(8,128)}, u32[]{:S(2)}) copy-start(f32[40,1280]{1,0:T(8,128)} %get-tuple-element.60) | copy-start | bytes 614404
  232.7 3.4 %copy-start.1 = (f32[40,1280]{1,0:T(8,128)S(1)}, f32[40,1280]{1,0:T(8,128)}, u32[]{:S(2)}) copy-start(f32[40,1280]{1,0:T(8,128)} %get-tuple-element.61) | copy-start | bytes 614404

commit v2 on v1

--- a/solution.py
+++ b/solution.py
@@ -359,9 +359,10 @@
 WIDTH = 1280
 SHARE = 40
 MINE = 320
-GROUP_HEADS = 4
 SLOTS = 1024
-PACK = 1024
+PACK = 512
+PAIR = 160
+COPIES = 144
 
 
 def fits(mesh):
@@ -384,8 +385,8 @@
     return pl.ds(pl.multiple_of(index * size, size), size)
 
 
-def strip(xx, yy):
-    return pl.ds(pl.multiple_of((xx * 2 + yy) * 2 * SHARE, 16), 2 * SHARE)
+def strip(yy):
+    return pl.ds(pl.multiple_of(yy * 2 * SHARE, 16), 2 * SHARE)
 
 
 def half(cc):
@@ -400,6 +401,7 @@
 
     def send(self, key, src, dst, device):
         index = self.count
+        assert index < COPIES
         self.count += 1
         copy = pltpu.make_async_remote_copy(
             src_ref=src,
@@ -419,6 +421,11 @@
     def sent(self, *keys):
         for key in keys:
             self.open.pop(key).wait_send()
+
+    def sent_of(self, name):
+        for key in list(self.open):
+            if key[0] == name:
+                self.open.pop(key).wait_send()
 
     def sent_all(self):
         for key in list(self.open):
@@ -494,6 +501,8 @@
     give_in,
     mix_send,
     mix_recv,
+    line_send,
+    line_recv,
     send_sems,
     recv_sems,
 ):
@@ -516,13 +525,16 @@
         pl.semaphore_signal(barrier, inc=1, device_id=device, device_id_type=MESH_ID)
 
     for member in range(4):
-        cols = slice(MINE * member, MINE * (member + 1))
-        stage[member] = jnp.concatenate(
-            [wq_ref[:, cols], wk_ref[:, cols], wv_ref[:, cols], jnp.zeros((SHARE, 64), BF16)], axis=1
-        )
-    qkv_own[s] = stage[s]
+        for p in range(2):
+            cols = slice(MINE * member + PAIR * p, MINE * member + PAIR * (p + 1))
+            stage[p, member] = jnp.concatenate(
+                [wq_ref[:, cols], wk_ref[:, cols], wv_ref[:, cols], jnp.zeros((SHARE, PACK - 3 * PAIR), BF16)],
+                axis=1,
+            )
+    for p in range(2):
+        qkv_own[p, s] = stage[p, s]
     tokens[s] = x_ref[...]
-    vec_slots[z, x, y, c] = vec_ref[...]
+    vec_slots[y, x, z, c] = vec_ref[...]
     shards = {"o": wo_ref, "h": wh_ref, "b": wb_ref}
     slot_of = {"o": 0, "h": 1, "b": 2}
     for m in "ohb":
@@ -531,135 +543,200 @@
 
     group = ((1, core_dev), (2, y_dev), (3, yc_dev))
     peers = (None, y * 2 + (1 - c), (1 - y) * 2 + c, (1 - y) * 2 + (1 - c))
-    for k, device in ((2, y_dev), (3, yc_dev), (1, core_dev)):
-        send(("a2a", k), stage.at[peers[k]], qkv_own.at[s], device)
+    def to_group(p):
+        for k, device in ((2, y_dev), (3, yc_dev), (1, core_dev)):
+            send(("a2a", p, k), stage.at[p, peers[k]], qkv_own.at[p, s], device)
+
+    fulls = {"o": full_o, "h": full_h, "b": full_b}
+    first_x = {"o": 1, "h": 0, "b": 1 - c}
+    far_x = {"b": 1 - c, "h": 1 - c, "o": c}
+
+    def spot(along, first, second):
+        on_x = along * first + (1 - along) * second
+        on_y = along * second + (1 - along) * first
+        return (x + on_x) % 2, strip((y + on_y) % 2)
+
+    def devs_of(along):
+        def device(on_x):
+            return ((z * 2 + (x + on_x) % 2), ((y + 1 - on_x) % 2) * 2 + c)
+
+        return device(along), device(1 - along)
+
+    up_dev = (jnp.minimum(z + 1, 3) * 2 + x, s)
+    down_dev = (jnp.maximum(z - 1, 0) * 2 + x, s)
+    streams = [0, 1] + [(m, e) for m in "ohb" for e in (0, 1)]
+
+    def line_piece(stream, zz, far):
+        if stream in (0, 1):
+            return qkv_w.at[stream, zz * 2 + (x + far) % 2]
+        m, e = stream
+        xx, rows = spot(first_x[m], e, far)
+        return fulls[m].at[zz, xx, rows, half(c)]
+
+    def line_copy(kind, stream, hop, zz, far=0):
+        if kind == 2:
+            device = x_dev if stream in (0, 1) else devs_of(first_x[stream[0]])[1]
+        else:
+            device = (up_dev, down_dev)[kind]
+        index = streams.index(stream)
+        piece = line_piece(stream, zz, far)
+        return pltpu.make_async_remote_copy(
+            src_ref=piece,
+            dst_ref=piece,
+            send_sem=line_send.at[kind, index, hop],
+            recv_sem=line_recv.at[kind, index, hop],
+            device_id=device,
+            device_id_type=MESH_ID,
+        )
+
+    def line_far(stream, zz):
+        line_copy(2, stream, zz, zz).start()
+
+    def line_first(stream):
+        @pl.when(z < 3)
+        def _():
+            line_copy(0, stream, 1, z).start()
+
+        @pl.when(z > 0)
+        def _():
+            line_copy(1, stream, 1, z).start()
+
+        line_far(stream, z)
+
+    def line_step(stream, hop):
+        @pl.when(z >= hop)
+        def _():
+            line_copy(0, stream, hop, z - hop).wait_recv()
+            if hop < 3:
+
+                @pl.when(z < 3)
+                def _():
+                    line_copy(0, stream, hop + 1, z - hop).start()
+
+            line_far(stream, z - hop)
+
+        @pl.when(z + hop <= 3)
+        def _():
+            line_copy(1, stream, hop, z + hop).wait_recv()
+            if hop < 3:
+
+                @pl.when(z > 0)
+                def _():
+                    line_copy(1, stream, hop + 1, z + hop).start()
+
+            line_far(stream, z + hop)
+
+    def line_done(stream):
+        for zz in range(4):
+            line_copy(2, stream, zz, zz, 1).wait_recv()
+
+    def line_sent(stream):
+        for hop in (1, 2, 3):
+
+            @pl.when((z >= hop - 1) & (z < 3))
+            def _():
+                line_copy(0, stream, hop, z).wait_send()
+
+            @pl.when((z + hop - 1 <= 3) & (z > 0))
+            def _():
+                line_copy(1, stream, hop, z).wait_send()
+
+        for zz in range(4):
+            line_copy(2, stream, zz, z).wait_send()
+
+    def to_core(m, far):
+        for e in (0, 1):
+            xx, rows = spot(first_x[m], e, far)
+            piece = fulls[m].at[:, xx, rows, half(c)]
+            send((m, far, e), piece, piece, core_dev)
+
+    def gather_side(m):
+        to_core(m, 0)
+
+    def gather_core(m):
+        line_done((m, 0))
+        line_done((m, 1))
+        to_core(m, 1)
+
+    def gather_done(m):
+        recv(*[(m, far, e) for far in (0, 1) for e in (0, 1)])
+
+    def own_rows(p):
+        recv(*[("a2a", p, k) for k in (1, 2, 3)])
+        qkv_w[p, d] = jnp.concatenate([qkv_own[p, member] for member in range(4)], axis=0)
+
+    def own_first(m):
+        recv(("pair", m))
+        piece = jnp.concatenate([pair_in[slot_of[m], 0], pair_in[slot_of[m], 1]], axis=0)
+        fulls[m][z, x, strip(y), half(c)] = piece
+        mine = fulls[m].at[z, x, strip(y), half(c)]
+        send((m, "first"), mine, mine, devs_of(first_x[m])[0])
+
+    to_group(0)
     for m in "ohb":
         send(("pair", m), shards[m].at[:, half(1 - c)], pair_in.at[slot_of[m], c], core_dev)
-    for k in (1, 2, 3):
-        send(("vz", k), vec_ref, vec_slots.at[z, x, y, c], z_devs[k])
+    send("vy", vec_ref, vec_slots.at[y, x, z, c], y_dev)
+    to_group(1)
+    own_first("o")
     send("xy", x_ref, tokens.at[s], y_dev)
     send("xc", x_ref, tokens.at[s], core_dev)
-
-    fulls = {"o": full_o, "h": full_h, "b": full_b}
-    near_axis = {"o": "x", "h": "x", "b": "y"}
-
-    def strip_of(axis, near, far):
-        if axis == "x":
-            return strip(x if near == 0 else 1 - x, y if far == 0 else 1 - y)
-        return strip(x if far == 0 else 1 - x, y if near == 0 else 1 - y)
-
-    def devs(m):
-        return (x_dev, y_dev) if near_axis[m] == "x" else (y_dev, x_dev)
-
-    def gather_z(m):
-        for k in (1, 2, 3):
-            piece = fulls[m].at[z, strip(x, y), half(c)]
-            send((m, "z", k), piece, piece, z_devs[k])
-
-    def gather_own(m):
-        near_dev, far_dev = devs(m)
-        piece = fulls[m].at[z, strip(x, y), half(c)]
-        send((m, "n", 0), piece, piece, near_dev)
-        send((m, "f", 0), piece, piece, far_dev)
-
-    def gather_near(m, k):
-        near_dev, far_dev = devs(m)
-        recv((m, "z", k))
-        piece = fulls[m].at[from_z[k], strip(x, y), half(c)]
-        send((m, "n", k), piece, piece, near_dev)
-        send((m, "f", k), piece, piece, far_dev)
-
-    def all_z(m, near, far):
-        return fulls[m].at[:, strip_of(near_axis[m], near, far), half(c)]
-
-    def gather_far(m):
-        near_dev, far_dev = devs(m)
-        piece = all_z(m, 0, 0)
-        send((m, "c", 0), piece, piece, core_dev)
-        recv(*[(m, "n", k) for k in range(4)])
-        piece = all_z(m, 1, 0)
-        send((m, "f", 4), piece, piece, far_dev)
-        send((m, "c", 1), piece, piece, core_dev)
-
-    def gather_core(m, part):
-        if part == 0:
-            recv(*[(m, "f", k) for k in range(4)])
-            piece = all_z(m, 0, 1)
-            send((m, "c", 2), piece, piece, core_dev)
-        else:
-            recv((m, "f", 4))
-            piece = all_z(m, 1, 1)
-            send((m, "c", 3), piece, piece, core_dev)
-
-    def gather_done(m):
-        recv(*[(m, "c", k) for k in range(4)])
-
-    for m in "ohb":
-        recv(("pair", m))
-        fulls[m][z, strip(x, y), half(c)] = jnp.concatenate(
-            [pair_in[slot_of[m], 0], pair_in[slot_of[m], 1]], axis=0
-        )
-    gather_z("o")
-    gather_own("o")
-    gather_own("h")
-    gather_own("b")
-    recv(("a2a", 1), ("a2a", 2), ("a2a", 3))
-    qkv_w[d] = jnp.concatenate([qkv_own[member] for member in range(4)], axis=0)
+    own_first("h")
+    own_first("b")
+    own_rows(0)
+    line_first(0)
+    recv("vy")
+    piece = vec_slots.at[:, x, z, c]
+    send("vx", piece, piece, x_dev)
+    line_first(("o", 0))
+    own_rows(1)
+    recv("vx")
     for k in (1, 2, 3):
-        send(("wz", k), qkv_w.at[d], qkv_w.at[d], z_devs[k])
-    send(("wx", 0), qkv_w.at[d], qkv_w.at[d], x_dev)
-    gather_z("h")
-    gather_z("b")
+        piece = vec_slots.at[:, :, z, c]
+        send(("vz", k), piece, piece, z_devs[k])
+    line_step(0, 1)
+    line_first(1)
+    line_step(0, 2)
     recv(("vz", 1), ("vz", 2), ("vz", 3))
-    piece = vec_slots.at[:, x, y, c]
-    send("vx", piece, piece, x_dev)
-    gather_near("o", 1)
-    gather_near("o", 2)
-    gather_near("o", 3)
-    recv("vx")
-    piece = vec_slots.at[:, :, y, c]
-    send("vy", piece, piece, y_dev)
-    recv("xy")
-    piece = tokens.at[peers[2]]
-    send("xyc", piece, piece, core_dev)
-    recv("vy")
     piece = vec_slots.at[:, :, :, c]
     send("vc", piece, piece, core_dev)
-
-    def qkv_near_step(k):
-        recv(("wz", k))
-        row = from_z[k] * 2 + x
-        send(("wx", k), qkv_w.at[row], qkv_w.at[row], x_dev)
-
-    gather_far("o")
-    qkv_near_step(1)
+    recv(("o", "first"))
+    line_first(("o", 1))
+    line_step(0, 3)
+    line_step(1, 1)
     recv("vc")
     vec_row[...] = jnp.zeros_like(vec_row)
     for slot in range(32):
         start = slot * SHARE
         low = start // 128 * 128
         piece = jnp.concatenate(
-            [vec_slots[slot // 8, slot // 4 % 2, slot // 2 % 2, slot % 2], jnp.zeros((8, 128), F32)], axis=1
+            [vec_slots[slot // 2 % 2, slot // 4 % 2, slot // 8, slot % 2], jnp.zeros((8, 128), F32)], axis=1
         )
         if start > low:
             piece = pltpu.roll(piece, start - low, 1)
         vec_row[:, low : low + 256] += piece
-    recv("xc", "xyc")
+
+    def norm_of(member, count):
+        def norm_rows(step, carry):
+            for j in range(count):
+                rows = tile(step, 64)
+                value = tokens[member + j, rows, :].astype(F32)
+                unit = value * lax.rsqrt(jnp.mean(value * value, axis=-1, keepdims=True) + 1e-06)
+                tokens[member + j, rows, :] = (unit * vec_row[0:1, :WIDTH]).astype(BF16)
+            return carry
+
+        lax.fori_loop(0, ROWS // 64, norm_rows, 0)
+
+    recv("xc")
+    norm_of(y * 2, 2)
+    line_step(("o", 0), 1)
+    recv("xy")
+    piece = tokens.at[peers[2]]
+    send("xyc", piece, piece, core_dev)
+    line_step(1, 2)
+    line_step(("o", 1), 1)
+    recv("xyc")
     links.sent("xyc")
-
-    def norm_rows(step, carry):
-        for member in range(4):
-            rows = tile(step, 64)
-            value = tokens[member, rows, :].astype(F32)
-            unit = value * lax.rsqrt(jnp.mean(value * value, axis=-1, keepdims=True) + 1e-06)
-            tokens[member, rows, :] = (unit * vec_row[0:1, :WIDTH]).astype(BF16)
-        return carry
-
-    lax.fori_loop(0, ROWS // 64, norm_rows, 0)
-    qkv_near_step(2)
-    gather_core("o", 0)
-    gather_core("o", 1)
-    qkv_near_step(3)
+    norm_of((1 - y) * 2, 2)
 
     def own(row):
         value = vec_row[row : row + 1, 0:MINE]
@@ -672,33 +749,33 @@
     scale = (jnp.maximum(query_log, 0.0) + jnp.log1p(jnp.exp(-jnp.abs(query_log)))) * factor
     query_bias, value_bias = own(1), own(3)
 
-    recv(*[("wx", k) for k in range(4)])
-    weights = qkv_w.reshape(WIDTH, PACK)
-
-    def project(i, carry):
-        rows = tile(i, ROWS)
-        raw = dot_nn(tokens[i], weights[...])
-        query = ((raw[:, :MINE] + query_bias) * scale).astype(BF16)
-        key = raw[:, MINE : 2 * MINE].astype(BF16)
-        val = (raw[:, 2 * MINE : 3 * MINE] + value_bias).astype(BF16)
-        queries_n[i] = query
-        queries_t[:, rows] = query.T
-        keys_t[:, rows] = key.T
-        vals_t[:, rows] = val.T
-        for h in range(GROUP_HEADS):
-            keys[h, rows, :] = key[:, HEAD_DIM * h : HEAD_DIM * (h + 1)]
-            vals[h, rows, :] = val[:, HEAD_DIM * h : HEAD_DIM * (h + 1)]
-        return carry
-
-    lax.fori_loop(0, 4, project, 0)
-    for k in (1, 2, 3):
-        gather_near("h", k)
+    weights = [qkv_w.at[p].reshape(WIDTH, PACK) for p in range(2)]
+
+    def project_pair(p):
+        lanes = slice(PAIR * p, PAIR * (p + 1))
+
+        def project(i, carry):
+            rows = tile(i, ROWS)
+            raw = dot_nn(tokens[i], weights[p][...])
+            query = ((raw[:, :PAIR] + query_bias[:, lanes]) * scale[:, lanes]).astype(BF16)
+            key = raw[:, PAIR : 2 * PAIR].astype(BF16)
+            val = (raw[:, 2 * PAIR : 3 * PAIR] + value_bias[:, lanes]).astype(BF16)
+            queries_n[p, i] = query
+            queries_t[lanes, rows] = query.T
+            keys_t[lanes, rows] = key.T
+            vals_t[lanes, rows] = val.T
+            for h in range(2):
+                keys[2 * p + h, rows, :] = key[:, HEAD_DIM * h : HEAD_DIM * (h + 1)]
+                vals[2 * p + h, rows, :] = val[:, HEAD_DIM * h : HEAD_DIM * (h + 1)]
+            return carry
+
+        lax.fori_loop(0, 4, project, 0)
 
     key_place = lax.broadcasted_iota(jnp.int32, (ROWS, ROWS), 0)
     query_place = lax.broadcasted_iota(jnp.int32, (ROWS, ROWS), 1)
     allowed = key_place <= query_place
 
-    def attend(i):
+    def attend(p, i):
         low, high = i * ROWS, (i + 1) * ROWS
 
         def head(h, carry):
@@ -720,40 +797,67 @@
             mix_out[i, rows, :] = (mixed / total).astype(BF16)
             return carry
 
-        lax.fori_loop(0, GROUP_HEADS, head, 0)
-
-    def mix_copy(dest, source):
+        lax.fori_loop(2 * p, 2 * p + 2, head, 0)
+
+    def mix_copy(p, dest, source):
         return pltpu.make_async_remote_copy(
-            src_ref=mix_out.at[dest],
-            dst_ref=mix_in.at[source],
-            send_sem=mix_send.at[dest],
-            recv_sem=mix_recv.at[source],
+            src_ref=mix_out.at[dest, PAIR * p : PAIR * (p + 1)],
+            dst_ref=mix_in.at[source, PAIR * p : PAIR * (p + 1)],
+            send_sem=mix_send.at[p, dest],
+            recv_sem=mix_recv.at[p, source],
             device_id=(d, dest),
             device_id_type=MESH_ID,
         )
 
-    for i in (3, 2, 1, 0):
-        attend(i)
+    def attend_and_send(p, i):
+        attend(p, i)
 
         @pl.when(s != i)
         def _():
-            mix_copy(i, s).start()
+            mix_copy(p, i, s).start()
 
         @pl.when(s == i)
         def _():
-            mix_in[i] = mix_out[i]
-
-        if i == 3:
-            gather_far("h")
-        if i == 2:
-            gather_near("b", 1)
-            gather_near("b", 2)
-        if i == 1:
-            gather_near("b", 3)
-
+            mix_in[i, PAIR * p : PAIR * (p + 1)] = mix_out[i, PAIR * p : PAIR * (p + 1)]
+
+    line_done(0)
+    project_pair(0)
+    line_step(1, 3)
+    line_step(("o", 0), 2)
+    attend_and_send(0, 3)
+    recv(("h", "first"))
+    line_first(("h", 0))
+    line_step(("o", 1), 2)
+    attend_and_send(0, 2)
+    line_first(("h", 1))
+    line_step(("o", 0), 3)
+    attend_and_send(0, 1)
+    line_step(("o", 1), 3)
+    gather_side("o")
+    attend_and_send(0, 0)
+    line_step(("h", 0), 1)
+    recv(("b", "first"))
+    line_first(("b", 0))
+    line_done(1)
+    project_pair(1)
+    line_step(("h", 1), 1)
+    line_first(("b", 1))
+    attend_and_send(1, 3)
+    line_step(("h", 0), 2)
+    line_step(("h", 1), 2)
+    gather_core("o")
+    attend_and_send(1, 2)
+    line_step(("b", 0), 1)
+    line_step(("b", 1), 1)
+    attend_and_send(1, 1)
+    line_step(("h", 0), 3)
+    line_step(("h", 1), 3)
+    attend_and_send(1, 0)
+    gather_side("h")
+    for p in range(2):
+        for k in (1, 2, 3):
+            mix_copy(p, peers[k], peers[k]).wait_recv()
     gather_done("o")
-    for k in (1, 2, 3):
-        mix_copy(peers[k], peers[k]).wait_recv()
 
     mix[...] = mix_in[...].reshape(WIDTH, ROWS).T
     mats = {m: fulls[m].reshape(WIDTH, WIDTH) for m in "ohb"}
@@ -775,9 +879,9 @@
         return carry
 
     lax.fori_loop(0, ROWS // 64, norm_two, 0)
-    gather_far("b")
-    gather_core("h", 0)
-    gather_core("h", 1)
+    line_step(("b", 0), 2)
+    line_step(("b", 1), 2)
+    gather_core("h")
     gather_done("h")
 
     def hidden_step(j, carry):
@@ -796,7 +900,6 @@
         return jnp.where(valid, cot_ref[...], jnp.zeros((ROWS, WIDTH), BF16))
 
     parts = {"b": part_b, "h": full_b, "o": full_h}
-    far_axis = {"b": "x", "h": "x", "o": "y"}
     outs = {"b": gb_ref, "h": gh_ref, "o": go_ref}
     order = {"b": 0, "h": 1, "o": 2}
 
@@ -810,14 +913,16 @@
 
         lax.fori_loop(0, 5, step, 0)
 
-    def part_at(m, far, near, cc):
-        return parts[m].at[:, strip_of(far_axis[m], far, near), half(cc)]
+    def part_at(m, far, near):
+        xx, rows = spot(far_x[m], far, near)
+        return parts[m].at[:, xx, rows, half(c)]
+
+    def part_for_core(m, far, near):
+        xx, rows = spot(1 - far_x[m], far, near)
+        return parts[m].at[:, xx, rows, half(1 - c)]
 
     def core_at(m, far, near):
-        ref = core_in.at[order[m]]
-        if far_axis[m] == "x":
-            return ref.at[:, x if far == 0 else 1 - x, y if near == 0 else 1 - y]
-        return ref.at[:, x if near == 0 else 1 - x, y if far == 0 else 1 - y]
+        return core_in.at[order[m], far, near]
 
     def add_into(target, other):
         def step(zz, carry):
@@ -827,54 +932,56 @@
         lax.fori_loop(0, 4, step, 0)
 
     def grad_devs(m):
-        return (x_dev, y_dev) if far_axis[m] == "x" else (y_dev, x_dev)
+        return devs_of(far_x[m])
 
     def scatter_core(m):
         for far in (1, 0):
             for near in (1, 0):
-                send((m, "gc", far, near), part_at(m, far, near, 1 - c), core_at(m, far, near), core_dev)
+                send(("gc", m, far, near), part_for_core(m, far, near), core_at(m, far, near), core_dev)
 
     def scatter_far(m):
         far_dev, near_dev = grad_devs(m)
         for near in (1, 0):
-            recv((m, "gc", 1, near))
-            add_into(part_at(m, 1, near, c), core_at(m, 1, near))
-            send((m, "gf", near), part_at(m, 1, near, c), far_in.at[order[m], near], far_dev)
+            recv(("gc", m, 1, near))
+            add_into(part_at(m, 1, near), core_at(m, 1, near))
+            send(("gf", m, near), part_at(m, 1, near), far_in.at[order[m], near], far_dev)
         for near in (1, 0):
-            recv((m, "gc", 0, near))
-            add_into(part_at(m, 0, near, c), core_at(m, 0, near))
+            recv(("gc", m, 0, near))
+            add_into(part_at(m, 0, near), core_at(m, 0, near))
 
     def scatter_near(m):
         far_dev, near_dev = grad_devs(m)
-        recv((m, "gf", 1))
-        add_into(part_at(m, 0, 1, c), far_in.at[order[m], 1])
-        send((m, "gn"), part_at(m, 0, 1, c), near_in.at[order[m]], near_dev)
-        recv((m, "gf", 0))
-        add_into(part_at(m, 0, 0, c), far_in.at[order[m], 0])
+        recv(("gf", m, 1))
+        add_into(part_at(m, 0, 1), far_in.at[order[m], 1])
+        send(("gn", m), part_at(m, 0, 1), near_in.at[order[m]], near_dev)
+        recv(("gf", m, 0))
+        add_into(part_at(m, 0, 0), far_in.at[order[m], 0])
 
     def scatter_z(m):
-        recv((m, "gn"))
-        add_into(part_at(m, 0, 0, c), near_in.at[order[m]])
+        recv(("gn", m))
+        add_into(part_at(m, 0, 0), near_in.at[order[m]])
         for k in (1, 2, 3):
-            send((m, "gz", k), part_at(m, 0, 0, c).at[zs[k]], last_in.at[order[m], k - 1], z_devs[k])
+            send(("gz", m, k), part_at(m, 0, 0).at[zs[k]], last_in.at[order[m], k - 1], z_devs[k])
 
     def scatter_sum(m):
-        total = part_at(m, 0, 0, c)[z].astype(F32)
+        total = part_at(m, 0, 0)[z].astype(F32)
         for k in (1, 2, 3):
-            recv((m, "gz", k))
+            recv(("gz", m, k))
             total += last_in[order[m], k - 1].astype(F32)
         outs[m][:, half(c)] = jnp.where(c == 0, total[:SHARE], total[SHARE:])
         give_out[order[m]] = jnp.where(c == 0, total[SHARE:], total[:SHARE])
-        send((m, "give"), give_out.at[order[m]], give_in.at[order[m]], core_dev)
+        send(("give", m), give_out.at[order[m]], give_in.at[order[m]], core_dev)
 
     def scatter_done(m):
-        recv((m, "give"))
+        recv(("give", m))
         outs[m][:, half(1 - c)] = give_in[order[m]]
 
     weight_grad("b", lambda j, right: dot_tn(active[:, tile(j, 256)], right))
     scatter_core("b")
-    gather_core("b", 0)
-    gather_core("b", 1)
+    line_step(("b", 0), 3)
+    line_step(("b", 1), 3)
+    gather_side("b")
+    gather_core("b")
     gather_done("b")
     scatter_far("b")
 
@@ -890,8 +997,9 @@
         return carry
 
     lax.fori_loop(0, 5, back_step, 0)
-    links.sent(*[("b", "c", k) for k in range(4)], *[("b", "z", k) for k in (1, 2, 3)])
-    links.sent(*[("b", kind, k) for kind in "nf" for k in range(4)], ("b", "f", 4))
+    links.sent_of("b")
+    line_sent(("b", 0))
+    line_sent(("b", 1))
     weight_grad("h", lambda j, right: dot_tn(norm2[:, tile(j, 256)], right))
     scatter_core("h")
 
@@ -924,18 +1032,19 @@
         return carry
 
     lax.fori_loop(0, 4, mixed_back, 0)
-    for k, device in ((2, y_dev), (3, yc_dev), (1, core_dev)):
-        send(("gm", k), gmix_out.at[peers[k]], gmix_in.at[s], device)
+    for p in range(2):
+        for k, device in ((2, y_dev), (3, yc_dev), (1, core_dev)):
+            rows = slice(PAIR * p, PAIR * (p + 1))
+            send(("gm", p, k), gmix_out.at[peers[k], rows], gmix_in.at[s, rows], device)
     gmix_in[s] = gmix_out[s]
     scatter_far("h")
-    links.sent(*[("h", "c", k) for k in range(4)], *[("h", "z", k) for k in (1, 2, 3)])
-    links.sent(*[("h", kind, k) for kind in "nf" for k in range(4)], ("h", "f", 4))
+    links.sent_of("h")
+    line_sent(("h", 0))
+    line_sent(("h", 1))
     mixed_flat = mix_in.reshape(WIDTH, ROWS)
     weight_grad("o", lambda j, right: dot_nn(mixed_flat[tile(j, 256), :], right))
     scatter_core("o")
     scatter_near("b")
-    recv(("gm", 1), ("gm", 2), ("gm", 3))
-    scatter_far("o")
 
     def attend_back(h):
         rows = slice(HEAD_DIM * h, HEAD_DIM * (h + 1))
@@ -964,71 +1073,109 @@
                 dk_acc[first:last, :] += dot_nt(grad_scores, query)
                 dv_acc[first:last, :] += dot_nt(probs.astype(BF16), grad)
             dq_t[rows, low:high] = grad_query
-        grads[:, MINE + HEAD_DIM * h : MINE + HEAD_DIM * (h + 1)] = dk_acc[...].astype(BF16)
-        grads[:, 2 * MINE + HEAD_DIM * h : 2 * MINE + HEAD_DIM * (h + 1)] = dv_acc[...].astype(BF16)
-
+        first = PAIR + HEAD_DIM * (h % 2)
+        grads[h // 2, :, first : first + HEAD_DIM] = dk_acc[...].astype(BF16)
+        grads[h // 2, :, first + PAIR : first + PAIR + HEAD_DIM] = dv_acc[...].astype(BF16)
+
+    def finish_pair(p):
+        lanes = slice(PAIR * p, PAIR * (p + 1))
+        pair_scale = scale[:, lanes]
+        bias_grad = jnp.zeros((1, PAIR), F32)
+        scale_grad = jnp.zeros((1, PAIR), F32)
+        value_grad = jnp.zeros((1, PAIR), F32)
+        grads[p, :, 3 * PAIR :] = jnp.zeros((SLOTS, PACK - 3 * PAIR), BF16)
+        for i in range(4):
+            rows = slice(i * ROWS, (i + 1) * ROWS)
+            grad = dq_t[lanes, rows].T
+            low_grad = (grad * pair_scale).astype(BF16)
+            grads[p, rows, 0:PAIR] = low_grad
+            bias_grad += jnp.sum(low_grad.astype(F32), axis=0, keepdims=True)
+            scale_grad += jnp.sum(grad * queries_n[p, i].astype(F32), axis=0, keepdims=True)
+            value_grad += jnp.sum(grads[p, rows, 2 * PAIR : 3 * PAIR].astype(F32), axis=0, keepdims=True)
+        scale_grad = scale_grad / pair_scale * jax.nn.sigmoid(query_log[:, lanes]) * factor
+        return bias_grad, scale_grad, value_grad
+
+    def qkv_grad_pair(p):
+        flat = qkv_part.at[p].reshape(WIDTH, PACK)
+
+        def qkv_grad(j, carry):
+            total = jnp.zeros((256, PACK), F32)
+            for i in range(4):
+                total += dot_tn(tokens[i, :, tile(j, 256)], grads[p, i * ROWS : (i + 1) * ROWS, :])
+            flat[tile(j, 256), :] = total.astype(BF16)
+            return carry
+
+        lax.fori_loop(0, 5, qkv_grad, 0)
+        for k in (1, 2, 3):
+            send(("px", p, k), qkv_part.at[p, zs[k], 1 - x], qkv_near.at[p, k], x_dev)
+        send(("px", p, 0), qkv_part.at[p, z, 1 - x], qkv_near.at[p, 0], x_dev)
+
+    def qkv_z(p, k):
+        recv(("px", p, k))
+        qkv_part[p, zs[k], x] = (qkv_part[p, zs[k], x].astype(F32) + qkv_near[p, k].astype(F32)).astype(BF16)
+        send(("pz", p, k), qkv_part.at[p, zs[k], x], qkv_last.at[p, k - 1], z_devs[k])
+
+    def qkv_sum_pair(p):
+        recv(("px", p, 0))
+        total = qkv_part[p, z, x].astype(F32) + qkv_near[p, 0].astype(F32)
+        for k in (1, 2, 3):
+            recv(("pz", p, k))
+            total += qkv_last[p, k - 1].astype(F32)
+        for member in range(4):
+            qkv_sum[p, member] = total[SHARE * member : SHARE * (member + 1), :].astype(BF16)
+        for k, device in ((2, y_dev), (3, yc_dev), (1, core_dev)):
+            send(("ph", p, k), qkv_sum.at[p, peers[k]], qkv_home.at[p, s], device)
+        qkv_home[p, s] = qkv_sum[p, s]
+
+    recv(("gm", 0, 1), ("gm", 0, 2), ("gm", 0, 3))
     attend_back(0)
+    scatter_far("o")
+    attend_back(1)
+    pair_grads = [finish_pair(0)]
+    qkv_grad_pair(0)
+    recv(("gm", 1, 1), ("gm", 1, 2), ("gm", 1, 3))
     scatter_near("h")
-    attend_back(1)
+    attend_back(2)
     scatter_z("b")
-    attend_back(2)
-    scatter_near("o")
+    qkv_z(0, 1)
     attend_back(3)
-    scatter_z("h")
-    grads[:, 3 * MINE :] = jnp.zeros((SLOTS, PACK - 3 * MINE), BF16)
-    bias_grad = jnp.zeros((1, MINE), F32)
-    scale_grad = jnp.zeros((1, MINE), F32)
-    value_grad = jnp.zeros((1, MINE), F32)
-    for i in range(4):
-        rows = slice(i * ROWS, (i + 1) * ROWS)
-        grad = dq_t[:, rows].T
-        low_grad = (grad * scale).astype(BF16)
-        grads[rows, 0:MINE] = low_grad
-        bias_grad += jnp.sum(low_grad.astype(F32), axis=0, keepdims=True)
-        scale_grad += jnp.sum(grad * queries_n[i].astype(F32), axis=0, keepdims=True)
-        value_grad += jnp.sum(grads[rows, 2 * MINE : 3 * MINE].astype(F32), axis=0, keepdims=True)
-    scale_grad = scale_grad / scale * jax.nn.sigmoid(query_log) * factor
-    for row, value in ((1, bias_grad), (2, scale_grad), (3, value_grad)):
-        vec_part[row : row + 1, :] = jnp.concatenate(
+    qkv_z(0, 2)
+    pair_grads.append(finish_pair(1))
+    qkv_grad_pair(1)
+    for row in range(3):
+        value = jnp.concatenate([pair_grads[0][row], pair_grads[1][row]], axis=1)
+        vec_part[row + 1 : row + 2, :] = jnp.concatenate(
             [jnp.where(s == member, value, 0.0) for member in range(4)], axis=1
         )
 
-    flat = qkv_part.reshape(WIDTH, PACK)
-
-    def qkv_grad(j, carry):
-        total = jnp.zeros((256, PACK), F32)
-        for i in range(4):
-            total += dot_tn(tokens[i, :, tile(j, 256)], grads[i * ROWS : (i + 1) * ROWS, :])
-        flat[tile(j, 256), :] = total.astype(BF16)
-        return carry
-
-    lax.fori_loop(0, 5, qkv_grad, 0)
-    for k in (1, 2, 3):
-        send(("px", k), qkv_part.at[zs[k], 1 - x], qkv_near.at[k], x_dev)
-    send(("px", 0), qkv_part.at[z, 1 - x], qkv_near.at[0], x_dev)
-
-    def unit_grad(j, carry):
-        cols = tile(j, 256)
-        for i in range(4):
-            tokens[i, :, cols] = dot_nt(grads[i * ROWS : (i + 1) * ROWS, :], weights[cols, :]).astype(BF16)
-        return carry
-
-    links.sent("xy", "xc")
-    lax.fori_loop(0, 5, unit_grad, 0)
-    for far in (1, 0):
-        member = (y if far == 0 else 1 - y) * 2 + (1 - c)
-        send(("uc", far), tokens.at[member], unit_core.at[far], core_dev)
+    def unit_rows(member):
+        def unit_grad(j, carry):
+            cols = tile(j, 256)
+            value = dot_nt(grads[0, tile(member, ROWS), :], weights[0][cols, :])
+            value += dot_nt(grads[1, tile(member, ROWS), :], weights[1][cols, :])
+            tokens[member, :, cols] = value.astype(BF16)
+            return carry
+
+        lax.fori_loop(0, 5, unit_grad, 0)
+
+    unit_rows((1 - y) * 2 + (1 - c))
+    send(("uc", 1), tokens.at[(1 - y) * 2 + (1 - c)], unit_core.at[1], core_dev)
+    far_member = (1 - y) * 2 + c
+    unit_rows(far_member)
     recv(("uc", 1))
-    far_member = (1 - y) * 2 + c
     tokens[far_member] = (tokens[far_member].astype(F32) + unit_core[1].astype(F32)).astype(BF16)
     send("uy", tokens.at[far_member], unit_far, y_dev)
+    unit_rows(y * 2 + (1 - c))
+    send(("uc", 0), tokens.at[y * 2 + (1 - c)], unit_core.at[0], core_dev)
+    unit_rows(s)
     recv(("uc", 0))
+    qkv_z(0, 3)
+    scatter_near("o")
+    scatter_z("h")
+    scatter_sum("b")
+    qkv_sum_pair(0)
     scatter_z("o")
-    for k in (1, 2, 3):
-        recv(("px", k))
-        qkv_part[zs[k], x] = (qkv_part[zs[k], x].astype(F32) + qkv_near[k].astype(F32)).astype(BF16)
-        send(("pz", k), qkv_part.at[zs[k], x], qkv_last.at[k - 1], z_devs[k])
-    scatter_sum("b")
+    qkv_z(1, 1)
     scatter_sum("h")
     recv("uy")
 
@@ -1046,49 +1193,60 @@
         return carry
 
     lax.fori_loop(0, ROWS // 64, input_back, 0)
-    send("sc", vec_part, vec_in.at[0], core_dev)
-    recv("sc")
-    links.sent("sc")
-    vec_part[...] += vec_in[0]
-    send("sy", vec_part, vec_in.at[1], y_dev)
+    for k, device in ((2, y_dev), (3, yc_dev), (1, core_dev)):
+        send(("sg", k), vec_part, vec_in.at[k - 1], device)
+    qkv_z(1, 2)
+    recv(("sg", 1), ("sg", 2), ("sg", 3))
+    links.sent(("sg", 1), ("sg", 2), ("sg", 3))
+    vec_part[...] += vec_in[0] + vec_in[1] + vec_in[2]
+    send("sx", vec_part, vec_in.at[3], x_dev)
+    qkv_z(1, 3)
     scatter_sum("o")
-    recv("sy")
-    links.sent("sy")
-    vec_part[...] += vec_in[1]
-    send("sx", vec_part, vec_in.at[2], x_dev)
     recv("sx")
     links.sent("sx")
-    vec_part[...] += vec_in[2]
+    vec_part[...] += vec_in[3]
     for k in (1, 2, 3):
-        send(("sz", k), vec_part, vec_in.at[2 + k], z_devs[k])
-    recv(("px", 0))
-    qkv_part[z, x] = (qkv_part[z, x].astype(F32) + qkv_near[0].astype(F32)).astype(BF16)
-    recv(("pz", 1), ("pz", 2), ("pz", 3))
-    total = qkv_part[z, x].astype(F32)
-    for k in (1, 2, 3):
-        total += qkv_last[k - 1].astype(F32)
-    for member in range(4):
-        qkv_sum[member] = total[SHARE * member : SHARE * (member + 1), :].astype(BF16)
-    for k, device in ((2, y_dev), (3, yc_dev), (1, core_dev)):
-        send(("ph", k), qkv_sum.at[peers[k]], qkv_home.at[s], device)
-    qkv_home[s] = qkv_sum[s]
+        send(("sz", k), vec_part, vec_in.at[3 + k], z_devs[k])
+    qkv_sum_pair(1)
     recv(("sz", 1), ("sz", 2), ("sz", 3))
-    total = vec_part[...] + vec_in[3] + vec_in[4] + vec_in[5]
+    total = vec_part[...] + vec_in[4] + vec_in[5] + vec_in[6]
     gvec_ref[...] = pltpu.roll(total, WIDTH - (d * 4 + s) * SHARE, 1)[:, :128]
     for m in "bho":
         scatter_done(m)
-    recv(("ph", 1), ("ph", 2), ("ph", 3))
-    for index, ref in enumerate((gq_ref, gk_ref, gv_ref)):
-        for member in range(4):
-            ref[:, MINE * member : MINE * (member + 1)] = qkv_home[
-                member, :, MINE * index : MINE * (index + 1)
-            ].astype(F32)
+    for p in range(2):
+        recv(("ph", p, 1), ("ph", p, 2), ("ph", p, 3))
+        for index, ref in enumerate((gq_ref, gk_ref, gv_ref)):
+            for member in range(4):
+                first = MINE * member + PAIR * p
+                ref[:, first : first + PAIR] = qkv_home[
+                    p, member, :, PAIR * index : PAIR * (index + 1)
+                ].astype(F32)
     links.sent_all()
-    for i in range(4):
-
-        @pl.when(s != i)
-        def _():
-            mix_copy(i, s).wait_send()
+    line_sent(("o", 0))
+    line_sent(("o", 1))
+    for p in range(2):
+        line_sent(p)
+        for i in range(4):
+
+            @pl.when(s != i)
+            def _():
+                mix_copy(p, i, s).wait_send()
+
+
+def finish_kernel(*refs):
+    sources, gvec, targets, held, sems = refs[:8], refs[8], refs[9:22], refs[22:30], refs[30]
+    places = (1, 0, 3, 6, 7, 9, 11, 12)
+    loads = [pltpu.make_async_copy(sources[i], held[i], sems.at[0, i]) for i in range(8)]
+    stores = [pltpu.make_async_copy(held[i], targets[places[i]], sems.at[1, i]) for i in range(8)]
+    for copy in loads:
+        copy.start()
+    for row, place in enumerate((2, 4, 5, 8, 10)):
+        targets[place][...] = gvec[row, :SHARE]
+    for load, store in zip(loads, stores):
+        load.wait()
+        store.start()
+    for copy in stores:
+        copy.wait()
 
 
 def fused_shards(
@@ -1107,29 +1265,31 @@
     w_hidden,
     w_back,
 ):
-    rows = jnp.stack([gain_attn, bias_query, query_scale, bias_value, gain_mlp]).astype(F32)
-    vectors = jnp.pad(rows, ((0, 3), (0, 128 - SHARE)))
+    vectors = sum(
+        jnp.pad(value.astype(F32)[None], ((row, 7 - row), (0, 128 - SHARE)))
+        for row, value in enumerate((gain_attn, bias_query, query_scale, bias_value, gain_mlp))
+    )
     vmem = pl.BlockSpec(memory_space=pltpu.VMEM)
-    whole = (4, 8 * SHARE, WIDTH)
+    whole = (4, 2, 4 * SHARE, WIDTH)
     buffers = [
         (whole, BF16),
         (whole, BF16),
         (whole, BF16),
         (whole, BF16),
-        ((3, 4, 2, 2, 2 * SHARE, WIDTH // 2), BF16),
+        ((3, 2, 2, 4, 2 * SHARE, WIDTH // 2), BF16),
         ((3, 2, 4, 2 * SHARE, WIDTH // 2), BF16),
         ((3, 4, 2 * SHARE, WIDTH // 2), BF16),
         ((3, 3, 2 * SHARE, WIDTH // 2), BF16),
-        ((8, 4 * SHARE, PACK), BF16),
-        ((4, SHARE, PACK), BF16),
+        ((2, 8, 4 * SHARE, PACK), BF16),
+        ((2, 4, SHARE, PACK), BF16),
         ((4, ROWS, WIDTH), BF16),
-        ((GROUP_HEADS, SLOTS, HEAD_DIM), BF16),
-        ((GROUP_HEADS, SLOTS, HEAD_DIM), BF16),
+        ((4, SLOTS, HEAD_DIM), BF16),
+        ((4, SLOTS, HEAD_DIM), BF16),
         ((MINE, SLOTS), BF16),
         ((MINE, SLOTS), BF16),
         ((MINE, SLOTS), BF16),
-        ((4, ROWS, MINE), BF16),
-        ((GROUP_HEADS, 1, SLOTS), F32),
+        ((2, 4, ROWS, PAIR), BF16),
+        ((4, 1, SLOTS), F32),
         ((4, MINE, ROWS), BF16),
         ((4, MINE, ROWS), BF16),
         ((ROWS, WIDTH), BF16),
@@ -1143,26 +1303,26 @@
         ((SLOTS, HEAD_DIM), F32),
         ((SLOTS, HEAD_DIM), F32),
         ((MINE, SLOTS), F32),
-        ((SLOTS, PACK), BF16),
+        ((2, SLOTS, PACK), BF16),
         ((2, ROWS, WIDTH), BF16),
         ((ROWS, WIDTH), BF16),
-        ((4, 2, 4 * SHARE, PACK), BF16),
-        ((4, 4 * SHARE, PACK), BF16),
-        ((3, 4 * SHARE, PACK), BF16),
-        ((4, SHARE, PACK), BF16),
-        ((4, SHARE, PACK), BF16),
-        ((4, 2, 2, 2, 8, 128), F32),
+        ((2, 4, 2, 4 * SHARE, PACK), BF16),
+        ((2, 4, 4 * SHARE, PACK), BF16),
+        ((2, 3, 4 * SHARE, PACK), BF16),
+        ((2, 4, SHARE, PACK), BF16),
+        ((2, 4, SHARE, PACK), BF16),
+        ((2, 2, 4, 2, 8, 128), F32),
         ((8, WIDTH + 128), F32),
         ((8, WIDTH), F32),
-        ((6, 8, WIDTH), F32),
-        ((4, SHARE, PACK), BF16),
+        ((7, 8, WIDTH), F32),
+        ((2, 4, SHARE, PACK), BF16),
         ((3, 2, SHARE, WIDTH // 2), BF16),
         ((3, SHARE, WIDTH // 2), F32),
         ((3, SHARE, WIDTH // 2), F32),
     ]
     scratch = [pltpu.VMEM(shape, kind) for shape, kind in buffers]
-    scratch += [pltpu.SemaphoreType.DMA((4,)), pltpu.SemaphoreType.DMA((4,))]
-    scratch += [pltpu.SemaphoreType.DMA((128,)), pltpu.SemaphoreType.DMA((128,))]
+    scratch += [pltpu.SemaphoreType.DMA((2, 4))] * 2 + [pltpu.SemaphoreType.DMA((3, 8, 4))] * 2
+    scratch += [pltpu.SemaphoreType.DMA((COPIES,))] * 2
     square = jax.ShapeDtypeStruct((SHARE, WIDTH), F32)
     results = pl.pallas_call(
         layer_kernel,
@@ -1197,21 +1357,21 @@
         w_back,
     )
     out, input_grad, gvec, gq, gk, gv, go, gh, gb = results
-    return (
-        out.reshape(inputs.shape),
-        input_grad.reshape(inputs.shape),
-        gvec[0, :SHARE],
-        gq,
-        gvec[1, :SHARE],
-        gvec[2, :SHARE],
-        gk,
-        gv,
-        gvec[3, :SHARE],
-        go,
-        gvec[4, :SHARE],
-        gh,
-        gb,
-    )
+    moved = (input_grad, out, gq, gk, gv, go, gh, gb)
+    anywhere = pl.BlockSpec(memory_space=pl.ANY)
+    vector = jax.ShapeDtypeStruct((SHARE,), F32)
+    shapes = [jax.ShapeDtypeStruct((ROWS, WIDTH), BF16), jax.ShapeDtypeStruct((ROWS, WIDTH), F32), vector, square]
+    shapes += [vector, vector, square, square, vector, square, vector, square, square]
+    done = pl.pallas_call(
+        finish_kernel,
+        out_shape=tuple(shapes),
+        in_specs=[anywhere] * 8 + [vmem],
+        out_specs=tuple(vmem if shape is vector else anywhere for shape in shapes),
+        scratch_shapes=[pltpu.VMEM(array.shape, array.dtype) for array in moved]
+        + [pltpu.SemaphoreType.DMA((2, 8))],
+        compiler_params=pltpu.CompilerParams(vmem_limit_bytes=66 * 1000 * 1000),
+    )(*moved, gvec)
+    return (done[0].reshape(inputs.shape), done[1].reshape(inputs.shape), *done[2:])
 
 
 def solution(mesh):

time: 238 us -> 194 us (0.82)
  Pallas kernels: 226 us -> 191 us
  local copies, waits for them, and re-layouts: 9.27 us -> 0 us
    pallas_call x1, Pallas kernels: 226 us -> 186 us  [fused_shards(): pl.pallas_call(layer_kernel, out_shape=(jax.ShapeDtypeStruct((ROWS, WIDTH...]
    unnamed x22 -> x0, local copies, waits for them, and re-layouts: 7.13 us -> none
    pallas_call x0 -> x1, Pallas kernels: none -> 4.33 us  [fused_shards(): pl.pallas_call(finish_kernel, out_shape=tuple(shapes), in_specs=[anywhere...]
where the time goes in v2:
time: 194 us; the launch traced here: 193 us
  Pallas kernels  191 us (98%)
    pallas_call x1, Pallas kernels, fused_shards(): pl.pallas_call(layer_kernel, out_shape=(jax.ShapeDtypeStruct((ROWS, WIDTH...  186 us
    pallas_call x1, Pallas kernels, fused_shards(): pl.pallas_call(finish_kernel, out_shape=tuple(shapes), in_specs=[anywhere...  4.33 us

profile of v2, /device:TPU:0, one launch (start us, length us, event | category | flops | bytes accessed | tf_op | source)
XLA Modules:
  0.0 193.4 jit_solution(7995785806974700808)
XLA Ops:
  1.3 1.3 convert_add_fusion.vec_ref
  2.6 186.3 %shard_map.237 = (bf16[256,1280]{1,0:T(8,128)(2,1)}, f32[256,1280]{1,0:T(8,128)}, f32[8,128]{1,0:T(8,128)}, f32[40,1280]{1,0:T(8,128)}, f32[40,1280]{1,0:T(8,128...) custom-call(bf16[256,1280]{1,0:T(8,128)(2,1)} %bitcast.15, ...), custom_call_target="tpu_custom_call" | custom-call | flops 24999999488 | bytes 10000000 | tf_op jit(solution)/shard_map/pallas_call | solution.py:1327
  188.9 4.3 %shard_map.238 = (bf16[256,1280]{1,0:T(8,128)(2,1)}, f32[256,1280]{1,0:T(8,128)}, f32[40]{0:T(128)}, f32[40,1280]{1,0:T(8,128)}, f32[40]{0:T(128)}, /*index=5*/f...) custom-call(f32[256,1280]{1,0:T(8,128)} %get-tuple-element.35.refs_0, ...), custom_call_target="tpu_custom_call" | custom-call | tf_op jit(solution)/shard_map/pallas_call | solution.py:1365

commit v3 on v2

--- a/solution.py
+++ b/solution.py
@@ -362,7 +362,7 @@
 SLOTS = 1024
 PACK = 512
 PAIR = 160
-COPIES = 144
+COPIES = 38
 
 
 def fits(mesh):
@@ -393,17 +393,28 @@
     return pl.ds(pl.multiple_of(cc * (WIDTH // 2), 128), WIDTH // 2)
 
 
+class Outputs:
+    def __init__(self, sems):
+        self.sems, self.open = sems, []
+
+    def start(self, held, target):
+        copy = pltpu.make_async_copy(held, target, self.sems.at[len(self.open)])
+        copy.start()
+        self.open.append(copy)
+
+    def wait(self):
+        for copy in self.open:
+            copy.wait()
+
+
 class Links:
-    def __init__(self, send_sems, recv_sems):
-        self.send_sems, self.recv_sems = send_sems, recv_sems
+    def __init__(self, send_sems, recv_sems, device):
+        self.send_sems, self.recv_sems, self.device = send_sems, recv_sems, device
         self.count = 0
         self.open = {}
 
-    def send(self, key, src, dst, device):
-        index = self.count
-        assert index < COPIES
-        self.count += 1
-        copy = pltpu.make_async_remote_copy(
+    def copy(self, index, src, dst, device):
+        return pltpu.make_async_remote_copy(
             src_ref=src,
             dst_ref=dst,
             send_sem=self.send_sems.at[index],
@@ -411,25 +422,39 @@
             device_id=device,
             device_id_type=MESH_ID,
         )
+
+    def next_index(self):
+        self.count += 1
+        assert self.count <= COPIES
+        return self.count - 1
+
+    def group(self, key, whole):
+        self.open[key] = self.copy(self.next_index(), whole, whole, self.device), self.count - 1
+
+    def send(self, key, src, dst, device, group=None):
+        if group is not None:
+            self.copy(self.open[group][1], src, dst, device).start()
+            return
+        index = self.next_index()
+        copy = self.copy(index, src, dst, device)
         copy.start()
-        self.open[key] = copy
+        self.open[key] = copy, index
 
     def recv(self, *keys):
         for key in keys:
-            self.open[key].wait_recv()
+            self.open[key][0].wait_recv()
 
     def sent(self, *keys):
         for key in keys:
-            self.open.pop(key).wait_send()
+            self.open.pop(key)[0].wait_send()
 
     def sent_of(self, name):
         for key in list(self.open):
             if key[0] == name:
-                self.open.pop(key).wait_send()
+                self.sent(key)
 
     def sent_all(self):
-        for key in list(self.open):
-            self.open.pop(key).wait_send()
+        self.sent(*list(self.open))
 
 
 def layer_kernel(
@@ -443,6 +468,15 @@
     wo_ref,
     wh_ref,
     wb_ref,
+    out_hbm,
+    ig_hbm,
+    gvec_hbm,
+    gq_hbm,
+    gk_hbm,
+    gv_hbm,
+    go_hbm,
+    gh_hbm,
+    gb_hbm,
     out_ref,
     ig_ref,
     gvec_ref,
@@ -458,7 +492,7 @@
     part_b,
     core_in,
     far_in,
-    near_in,
+    line_in,
     last_in,
     qkv_w,
     stage,
@@ -477,7 +511,6 @@
     hidden,
     norm2,
     active,
-    gmix_out,
     gmix_in,
     grad_low,
     dk_acc,
@@ -488,9 +521,8 @@
     unit_far,
     qkv_part,
     qkv_near,
-    qkv_last,
+    qkv_line,
     qkv_home,
-    qkv_sum,
     vec_slots,
     vec_row,
     vec_part,
@@ -499,10 +531,14 @@
     pair_in,
     give_out,
     give_in,
+    out_sems,
     mix_send,
     mix_recv,
     line_send,
     line_recv,
+    sum_send,
+    sum_recv,
+    far_recv,
     send_sems,
     recv_sems,
 ):
@@ -510,9 +546,10 @@
     s = lax.axis_index("seq")
     z, x = d // 2, d % 2
     y, c = s // 2, s % 2
-    links = Links(send_sems, recv_sems)
+    results = Outputs(out_sems)
+    core_dev = (d, y * 2 + (1 - c))
+    links = Links(send_sems, recv_sems, core_dev)
     send, recv = links.send, links.recv
-    core_dev = (d, y * 2 + (1 - c))
     y_dev = (d, (1 - y) * 2 + c)
     yc_dev = (d, (1 - y) * 2 + (1 - c))
     x_dev = (z * 2 + (1 - x), s)
@@ -544,12 +581,14 @@
     group = ((1, core_dev), (2, y_dev), (3, yc_dev))
     peers = (None, y * 2 + (1 - c), (1 - y) * 2 + c, (1 - y) * 2 + (1 - c))
     def to_group(p):
+        links.group(("a2a", p), qkv_own.at[p, pl.ds(0, 3)])
         for k, device in ((2, y_dev), (3, yc_dev), (1, core_dev)):
-            send(("a2a", p, k), stage.at[p, peers[k]], qkv_own.at[p, s], device)
+            send(None, stage.at[p, peers[k]], qkv_own.at[p, s], device, ("a2a", p))
 
     fulls = {"o": full_o, "h": full_h, "b": full_b}
     first_x = {"o": 1, "h": 0, "b": 1 - c}
-    far_x = {"b": 1 - c, "h": 1 - c, "o": c}
+    last_x = {"b": c, "h": c, "o": 1}
+    last_x_other = {"b": 1 - c, "h": 1 - c, "o": 1}
 
     def spot(along, first, second):
         on_x = along * first + (1 - along) * second
@@ -573,19 +612,33 @@
         xx, rows = spot(first_x[m], e, far)
         return fulls[m].at[zz, xx, rows, half(c)]
 
-    def line_copy(kind, stream, hop, zz, far=0):
+    def line_copy(kind, stream, hop, zz):
         if kind == 2:
             device = x_dev if stream in (0, 1) else devs_of(first_x[stream[0]])[1]
         else:
             device = (up_dev, down_dev)[kind]
         index = streams.index(stream)
-        piece = line_piece(stream, zz, far)
+        piece = line_piece(stream, zz, 0)
         return pltpu.make_async_remote_copy(
             src_ref=piece,
             dst_ref=piece,
-            send_sem=line_send.at[kind, index, hop],
-            recv_sem=line_recv.at[kind, index, hop],
+            send_sem=line_send.at[kind, index],
+            recv_sem=far_recv.at[0, index] if kind == 2 else line_recv.at[kind, index, hop - 1],
             device_id=device,
+            device_id_type=MESH_ID,
+        )
+
+    def pieces(stream, count, sends, recvs):
+        if stream in (0, 1):
+            whole = qkv_w.at[stream, pl.ds(0, count)]
+        else:
+            whole = fulls[stream[0]].at[pl.ds(0, count), 0, pl.ds(0, 2 * SHARE), half(c)]
+        return pltpu.make_async_remote_copy(
+            src_ref=whole,
+            dst_ref=whole,
+            send_sem=sends,
+            recv_sem=recvs,
+            device_id=core_dev,
             device_id_type=MESH_ID,
         )
 
@@ -627,28 +680,30 @@
             line_far(stream, z + hop)
 
     def line_done(stream):
-        for zz in range(4):
-            line_copy(2, stream, zz, zz, 1).wait_recv()
+        index = streams.index(stream)
+        pieces(stream, 4, line_send.at[2, index], far_recv.at[0, index]).wait_recv()
 
     def line_sent(stream):
-        for hop in (1, 2, 3):
-
-            @pl.when((z >= hop - 1) & (z < 3))
+        index = streams.index(stream)
+        for zz in range(3):
+
+            @pl.when(z == zz)
             def _():
-                line_copy(0, stream, hop, z).wait_send()
-
-            @pl.when((z + hop - 1 <= 3) & (z > 0))
+                pieces(stream, zz + 1, line_send.at[0, index], far_recv.at[0, index]).wait_send()
+
+            @pl.when(z == zz + 1)
             def _():
-                line_copy(1, stream, hop, z).wait_send()
-
-        for zz in range(4):
-            line_copy(2, stream, zz, z).wait_send()
+                pieces(stream, 3 - zz, line_send.at[1, index], far_recv.at[0, index]).wait_send()
+
+        pieces(stream, 4, line_send.at[2, index], far_recv.at[0, index]).wait_send()
 
     def to_core(m, far):
+        if far == 0:
+            links.group((m, "c"), fulls[m].at[:, :, :, half(c)])
         for e in (0, 1):
             xx, rows = spot(first_x[m], e, far)
             piece = fulls[m].at[:, xx, rows, half(c)]
-            send((m, far, e), piece, piece, core_dev)
+            send(None, piece, piece, core_dev, (m, "c"))
 
     def gather_side(m):
         to_core(m, 0)
@@ -659,22 +714,24 @@
         to_core(m, 1)
 
     def gather_done(m):
-        recv(*[(m, far, e) for far in (0, 1) for e in (0, 1)])
+        recv((m, "c"))
 
     def own_rows(p):
-        recv(*[("a2a", p, k) for k in (1, 2, 3)])
+        recv(("a2a", p))
         qkv_w[p, d] = jnp.concatenate([qkv_own[p, member] for member in range(4)], axis=0)
 
     def own_first(m):
-        recv(("pair", m))
+        if m == "o":
+            recv("pair")
         piece = jnp.concatenate([pair_in[slot_of[m], 0], pair_in[slot_of[m], 1]], axis=0)
         fulls[m][z, x, strip(y), half(c)] = piece
         mine = fulls[m].at[z, x, strip(y), half(c)]
         send((m, "first"), mine, mine, devs_of(first_x[m])[0])
 
     to_group(0)
+    links.group("pair", pair_in.at[:, 0])
     for m in "ohb":
-        send(("pair", m), shards[m].at[:, half(1 - c)], pair_in.at[slot_of[m], c], core_dev)
+        send(None, shards[m].at[:, half(1 - c)], pair_in.at[slot_of[m], c], core_dev, "pair")
     send("vy", vec_ref, vec_slots.at[y, x, z, c], y_dev)
     to_group(1)
     own_first("o")
@@ -690,13 +747,14 @@
     line_first(("o", 0))
     own_rows(1)
     recv("vx")
+    links.group("vz", vec_slots.at[:, :, pl.ds(0, 3), c])
     for k in (1, 2, 3):
         piece = vec_slots.at[:, :, z, c]
-        send(("vz", k), piece, piece, z_devs[k])
+        send(None, piece, piece, z_devs[k], "vz")
     line_step(0, 1)
     line_first(1)
     line_step(0, 2)
-    recv(("vz", 1), ("vz", 2), ("vz", 3))
+    recv("vz")
     piece = vec_slots.at[:, :, :, c]
     send("vc", piece, piece, core_dev)
     recv(("o", "first"))
@@ -803,8 +861,8 @@
         return pltpu.make_async_remote_copy(
             src_ref=mix_out.at[dest, PAIR * p : PAIR * (p + 1)],
             dst_ref=mix_in.at[source, PAIR * p : PAIR * (p + 1)],
-            send_sem=mix_send.at[p, dest],
-            recv_sem=mix_recv.at[p, source],
+            send_sem=mix_send,
+            recv_sem=mix_recv,
             device_id=(d, dest),
             device_id_type=MESH_ID,
         )
@@ -854,9 +912,15 @@
     line_step(("h", 1), 3)
     attend_and_send(1, 0)
     gather_side("h")
-    for p in range(2):
-        for k in (1, 2, 3):
-            mix_copy(p, peers[k], peers[k]).wait_recv()
+    mix_whole = pltpu.make_async_remote_copy(
+        src_ref=mix_in.at[pl.ds(0, 3)],
+        dst_ref=mix_in.at[pl.ds(0, 3)],
+        send_sem=mix_send,
+        recv_sem=mix_recv,
+        device_id=core_dev,
+        device_id_type=MESH_ID,
+    )
+    mix_whole.wait_recv()
     gather_done("o")
 
     mix[...] = mix_in[...].reshape(WIDTH, ROWS).T
@@ -899,13 +963,14 @@
     def grad_y():
         return jnp.where(valid, cot_ref[...], jnp.zeros((ROWS, WIDTH), BF16))
 
-    parts = {"b": part_b, "h": full_b, "o": full_h}
+    parts = {"b": part_b, "h": full_h, "o": full_b}
     outs = {"b": gb_ref, "h": gh_ref, "o": go_ref}
+    outs_hbm = {"b": gb_hbm, "h": gh_hbm, "o": go_hbm}
     order = {"b": 0, "h": 1, "o": 2}
 
     def weight_grad(m, left):
         flat = parts[m].reshape(WIDTH, WIDTH)
-        right = grad_y() if m == "b" else grad_low[...]
+        right = {"b": grad_y, "h": lambda: mix[...], "o": lambda: grad_low[...]}[m]()
 
         def step(j, carry):
             flat[tile(j, 256), :] = left(j, right).astype(BF16)
@@ -913,61 +978,168 @@
 
         lax.fori_loop(0, 5, step, 0)
 
-    def part_at(m, far, near):
-        xx, rows = spot(far_x[m], far, near)
+    def sum_piece(stream, zz, far):
+        if stream in (0, 1):
+            return qkv_part.at[stream, zz, (x + far) % 2]
+        m, e = stream
+        xx, rows = spot(last_x[m], e, far)
+        return parts[m].at[zz, xx, rows, half(c)]
+
+    def sum_in(kind, stream, zz):
+        if stream in (0, 1):
+            return qkv_near.at[stream, zz] if kind == 2 else qkv_line.at[kind, stream, zz - 1 + kind]
+        index = streams.index(stream) - 2
+        return far_in.at[index, zz] if kind == 2 else line_in.at[kind, index, zz - 1 + kind]
+
+    def sum_copy(kind, stream, zz):
+        if kind == 2:
+            device = x_dev if stream in (0, 1) else devs_of(last_x[stream[0]])[1]
+        else:
+            device = (up_dev, down_dev)[kind]
+        index = streams.index(stream)
+        return pltpu.make_async_remote_copy(
+            src_ref=sum_piece(stream, zz, kind // 2),
+            dst_ref=sum_in(kind, stream, zz),
+            send_sem=sum_send.at[kind, index],
+            recv_sem=far_recv.at[1, index] if kind == 2 else sum_recv.at[kind, index, zz - 1 + kind],
+            device_id=device,
+            device_id_type=MESH_ID,
+        )
+
+    def add_in(kind, stream, zz):
+        if kind < 2:
+            sum_copy(kind, stream, zz).wait_recv()
+        piece = sum_piece(stream, zz, 0)
+        piece[...] = (piece[...].astype(F32) + sum_in(kind, stream, zz)[...].astype(F32)).astype(BF16)
+
+    def add_far(stream):
+        index = streams.index(stream)
+        pieces(stream, 4, sum_send.at[2, index], far_recv.at[1, index]).wait_recv()
+        for zz in range(4):
+            add_in(2, stream, zz)
+
+    def sum_far(stream):
+        for zz in (3, 0, 2, 1):
+            sum_copy(2, stream, zz).start()
+
+    def sum_step(stream, step):
+        if step == 0:
+            add_far(stream)
+        above, below = z + 3 - step, z + step - 3
+
+        @pl.when((z >= 1) & (z <= step))
+        def _():
+            add_in(0, stream, above)
+
+        @pl.when((z <= 2) & (3 - z <= step))
+        def _():
+            add_in(1, stream, below)
+
+        if step < 3:
+
+            @pl.when((z <= step) & (z > 0))
+            def _():
+                sum_copy(0, stream, above).start()
+
+            @pl.when((3 - z <= step) & (z < 3))
+            def _():
+                sum_copy(1, stream, below).start()
+
+        if step == 0:
+            @pl.when(z == 0)
+            def _():
+                for zz in (3, 2, 1):
+                    sum_copy(0, stream, zz).start()
+
+            @pl.when(z == 3)
+            def _():
+                for zz in (0, 1, 2):
+                    sum_copy(1, stream, zz).start()
+
+    direct = (1,)
+
+    def direct_copy(stream, k):
+        index = streams.index(stream)
+        return pltpu.make_async_remote_copy(
+            src_ref=sum_piece(stream, zs[k], 0),
+            dst_ref=sum_in(0, stream, k),
+            send_sem=sum_send.at[0, index],
+            recv_sem=sum_recv.at[0, index, 0],
+            device_id=z_devs[k],
+            device_id_type=MESH_ID,
+        )
+
+    def direct_start(stream):
+        add_far(stream)
+        for k in (2, 1, 3):
+            direct_copy(stream, k).start()
+
+    def direct_done(stream):
+        total = sum_piece(stream, z, 0)[...].astype(F32)
+        index = streams.index(stream)
+        pieces(stream, 3, sum_send.at[0, index], sum_recv.at[0, index, 0]).wait_recv()
+        for k in (1, 2, 3):
+            total += sum_in(0, stream, k)[...].astype(F32)
+        sum_piece(stream, z, 0)[...] = total.astype(BF16)
+
+    def sum_sent(stream):
+        index = streams.index(stream)
+        recvs = far_recv.at[1, index]
+        if stream in direct:
+            pieces(stream, 3, sum_send.at[0, index], recvs).wait_send()
+        else:
+            for zz in range(3):
+
+                @pl.when(z == zz)
+                def _():
+                    pieces(stream, 3 - zz, sum_send.at[0, index], recvs).wait_send()
+
+                @pl.when(z == zz + 1)
+                def _():
+                    pieces(stream, zz + 1, sum_send.at[1, index], recvs).wait_send()
+
+        pieces(stream, 4, sum_send.at[2, index], recvs).wait_send()
+
+    def core_piece(m, far, e):
+        xx, rows = spot(last_x[m], e, far)
         return parts[m].at[:, xx, rows, half(c)]
 
-    def part_for_core(m, far, near):
-        xx, rows = spot(1 - far_x[m], far, near)
-        return parts[m].at[:, xx, rows, half(1 - c)]
-
-    def core_at(m, far, near):
-        return core_in.at[order[m], far, near]
-
-    def add_into(target, other):
+    def scatter_core(m):
+        for far in (1, 0):
+            links.group(("gc", m, far), core_in.at[order[m], far])
+            for e in (0, 1):
+                xx, rows = spot(last_x_other[m], e, far)
+                piece = parts[m].at[:, xx, rows, half(1 - c)]
+                send(None, piece, core_in.at[order[m], far, e], core_dev, ("gc", m, far))
+
+    def core_add(m, far, e):
+        if e == 0:
+            recv(("gc", m, far))
+        target, other = core_piece(m, far, e), core_in.at[order[m], far, e]
+
         def step(zz, carry):
             target[zz] = (target[zz].astype(F32) + other[zz].astype(F32)).astype(BF16)
             return carry
 
         lax.fori_loop(0, 4, step, 0)
 
-    def grad_devs(m):
-        return devs_of(far_x[m])
-
-    def scatter_core(m):
-        for far in (1, 0):
-            for near in (1, 0):
-                send(("gc", m, far, near), part_for_core(m, far, near), core_at(m, far, near), core_dev)
-
     def scatter_far(m):
-        far_dev, near_dev = grad_devs(m)
-        for near in (1, 0):
-            recv(("gc", m, 1, near))
-            add_into(part_at(m, 1, near), core_at(m, 1, near))
-            send(("gf", m, near), part_at(m, 1, near), far_in.at[order[m], near], far_dev)
-        for near in (1, 0):
-            recv(("gc", m, 0, near))
-            add_into(part_at(m, 0, near), core_at(m, 0, near))
-
-    def scatter_near(m):
-        far_dev, near_dev = grad_devs(m)
-        recv(("gf", m, 1))
-        add_into(part_at(m, 0, 1), far_in.at[order[m], 1])
-        send(("gn", m), part_at(m, 0, 1), near_in.at[order[m]], near_dev)
-        recv(("gf", m, 0))
-        add_into(part_at(m, 0, 0), far_in.at[order[m], 0])
-
-    def scatter_z(m):
-        recv(("gn", m))
-        add_into(part_at(m, 0, 0), near_in.at[order[m]])
-        for k in (1, 2, 3):
-            send(("gz", m, k), part_at(m, 0, 0).at[zs[k]], last_in.at[order[m], k - 1], z_devs[k])
+        for e in (0, 1):
+            core_add(m, 1, e)
+            sum_far((m, e))
+        for e in (0, 1):
+            core_add(m, 0, e)
+
+    def both(m, step):
+        sum_step((m, 0), step)
+        sum_step((m, 1), step)
+
+    def scatter_last(m):
+        send(("gl", m), sum_piece((m, 1), z, 0), last_in.at[order[m]], devs_of(last_x[m])[0])
 
     def scatter_sum(m):
-        total = part_at(m, 0, 0)[z].astype(F32)
-        for k in (1, 2, 3):
-            recv(("gz", m, k))
-            total += last_in[order[m], k - 1].astype(F32)
+        recv(("gl", m))
+        total = sum_piece((m, 0), z, 0)[...].astype(F32) + last_in[order[m]].astype(F32)
         outs[m][:, half(c)] = jnp.where(c == 0, total[:SHARE], total[SHARE:])
         give_out[order[m]] = jnp.where(c == 0, total[SHARE:], total[:SHARE])
         send(("give", m), give_out.at[order[m]], give_in.at[order[m]], core_dev)
@@ -975,15 +1147,16 @@
     def scatter_done(m):
         recv(("give", m))
         outs[m][:, half(1 - c)] = give_in[order[m]]
+        results.start(outs[m], outs_hbm[m])
 
     weight_grad("b", lambda j, right: dot_tn(active[:, tile(j, 256)], right))
     scatter_core("b")
     line_step(("b", 0), 3)
     line_step(("b", 1), 3)
     gather_side("b")
+    scatter_far("b")
     gather_core("b")
     gather_done("b")
-    scatter_far("b")
 
     def back_step(j, carry):
         cols = tile(j, 256)
@@ -991,23 +1164,22 @@
         sigma = jax.nn.sigmoid(value)
         grad = dot_nt(grad_y(), mats["b"][cols, :])
         grad_low[:, cols] = (grad * sigma * (1.0 + value * (1.0 - sigma))).astype(BF16)
-        out_ref[:, cols] = jnp.where(
-            valid, middle[:, cols] + dot_nn(active[...], mats["b"][:, cols]), 0.0
-        ).astype(BF16)
         return carry
 
     lax.fori_loop(0, 5, back_step, 0)
-    links.sent_of("b")
-    line_sent(("b", 0))
-    line_sent(("b", 1))
-    weight_grad("h", lambda j, right: dot_tn(norm2[:, tile(j, 256)], right))
-    scatter_core("h")
+    mix[...] = grad_low[...]
 
     def normed_step(j, carry):
         hidden[:, tile(j, 256)] = dot_nt(grad_low[...], mats["h"][tile(j, 256), :])
         return carry
 
     lax.fori_loop(0, 5, normed_step, 0)
+    links.sent_of("h")
+    line_sent(("h", 0))
+    line_sent(("h", 1))
+    weight_grad("h", lambda j, right: dot_tn(norm2[:, tile(j, 256)], right))
+    scatter_core("h")
+    both("b", 0)
     vec_part[...] = jnp.zeros_like(vec_part)
 
     def middle_back(step, carry):
@@ -1027,24 +1199,35 @@
 
     lax.fori_loop(0, ROWS // 64, middle_back, 0)
 
+    mix_whole.wait_send()
+
     def mixed_back(member, carry):
-        gmix_out[member] = dot_nt(mats["o"][tile(member, MINE), :], grad_low[...]).astype(BF16)
+        mix_out[member] = dot_nt(mats["o"][tile(member, MINE), :], grad_low[...]).astype(BF16)
         return carry
 
     lax.fori_loop(0, 4, mixed_back, 0)
     for p in range(2):
+        rows = slice(PAIR * p, PAIR * (p + 1))
+        links.group(("gm", p), gmix_in.at[pl.ds(0, 3), rows])
         for k, device in ((2, y_dev), (3, yc_dev), (1, core_dev)):
-            rows = slice(PAIR * p, PAIR * (p + 1))
-            send(("gm", p, k), gmix_out.at[peers[k], rows], gmix_in.at[s, rows], device)
-    gmix_in[s] = gmix_out[s]
+            send(None, mix_out.at[peers[k], rows], gmix_in.at[s, rows], device, ("gm", p))
+    gmix_in[s] = mix_out[s]
     scatter_far("h")
-    links.sent_of("h")
-    line_sent(("h", 0))
-    line_sent(("h", 1))
+
+    def out_step(j, carry):
+        cols = tile(j, 256)
+        value = middle[:, cols] + dot_nn(active[...], mats["b"][:, cols])
+        out_ref[:, cols] = jnp.where(valid, value, 0.0).astype(BF16)
+        return carry
+
+    lax.fori_loop(0, 5, out_step, 0)
+    results.start(out_ref, out_hbm)
+    links.sent_of("b")
+    line_sent(("b", 0))
+    line_sent(("b", 1))
     mixed_flat = mix_in.reshape(WIDTH, ROWS)
     weight_grad("o", lambda j, right: dot_nn(mixed_flat[tile(j, 256), :], right))
     scatter_core("o")
-    scatter_near("b")
 
     def attend_back(h):
         rows = slice(HEAD_DIM * h, HEAD_DIM * (h + 1))
@@ -1072,7 +1255,7 @@
                 grad_query += dot_nn(keys_t[rows, first:last], grad_scores)
                 dk_acc[first:last, :] += dot_nt(grad_scores, query)
                 dv_acc[first:last, :] += dot_nt(probs.astype(BF16), grad)
-            dq_t[rows, low:high] = grad_query
+            dq_t[HEAD_DIM * (h % 2) : HEAD_DIM * (h % 2 + 1), low:high] = grad_query
         first = PAIR + HEAD_DIM * (h % 2)
         grads[h // 2, :, first : first + HEAD_DIM] = dk_acc[...].astype(BF16)
         grads[h // 2, :, first + PAIR : first + PAIR + HEAD_DIM] = dv_acc[...].astype(BF16)
@@ -1086,7 +1269,7 @@
         grads[p, :, 3 * PAIR :] = jnp.zeros((SLOTS, PACK - 3 * PAIR), BF16)
         for i in range(4):
             rows = slice(i * ROWS, (i + 1) * ROWS)
-            grad = dq_t[lanes, rows].T
+            grad = dq_t[:, rows].T
             low_grad = (grad * pair_scale).astype(BF16)
             grads[p, rows, 0:PAIR] = low_grad
             bias_grad += jnp.sum(low_grad.astype(F32), axis=0, keepdims=True)
@@ -1106,42 +1289,38 @@
             return carry
 
         lax.fori_loop(0, 5, qkv_grad, 0)
-        for k in (1, 2, 3):
-            send(("px", p, k), qkv_part.at[p, zs[k], 1 - x], qkv_near.at[p, k], x_dev)
-        send(("px", p, 0), qkv_part.at[p, z, 1 - x], qkv_near.at[p, 0], x_dev)
-
-    def qkv_z(p, k):
-        recv(("px", p, k))
-        qkv_part[p, zs[k], x] = (qkv_part[p, zs[k], x].astype(F32) + qkv_near[p, k].astype(F32)).astype(BF16)
-        send(("pz", p, k), qkv_part.at[p, zs[k], x], qkv_last.at[p, k - 1], z_devs[k])
+        sum_far(p)
 
     def qkv_sum_pair(p):
-        recv(("px", p, 0))
-        total = qkv_part[p, z, x].astype(F32) + qkv_near[p, 0].astype(F32)
-        for k in (1, 2, 3):
-            recv(("pz", p, k))
-            total += qkv_last[p, k - 1].astype(F32)
+        links.sent(("a2a", p))
+        if p in direct:
+            direct_done(p)
+        total = qkv_part[p, z, x].astype(F32)
         for member in range(4):
-            qkv_sum[p, member] = total[SHARE * member : SHARE * (member + 1), :].astype(BF16)
+            stage[p, member] = total[SHARE * member : SHARE * (member + 1), :].astype(BF16)
+        links.group(("ph", p), qkv_home.at[p, pl.ds(0, 3)])
         for k, device in ((2, y_dev), (3, yc_dev), (1, core_dev)):
-            send(("ph", p, k), qkv_sum.at[p, peers[k]], qkv_home.at[p, s], device)
-        qkv_home[p, s] = qkv_sum[p, s]
-
-    recv(("gm", 0, 1), ("gm", 0, 2), ("gm", 0, 3))
+            send(None, stage.at[p, peers[k]], qkv_home.at[p, s], device, ("ph", p))
+        qkv_home[p, s] = stage[p, s]
+
+    both("b", 1)
+    recv(("gm", 0))
     attend_back(0)
     scatter_far("o")
+    both("b", 2)
     attend_back(1)
     pair_grads = [finish_pair(0)]
     qkv_grad_pair(0)
-    recv(("gm", 1, 1), ("gm", 1, 2), ("gm", 1, 3))
-    scatter_near("h")
+    both("b", 3)
+    scatter_last("b")
+    both("h", 0)
+    recv(("gm", 1))
     attend_back(2)
-    scatter_z("b")
-    qkv_z(0, 1)
     attend_back(3)
-    qkv_z(0, 2)
+    both("h", 1)
     pair_grads.append(finish_pair(1))
     qkv_grad_pair(1)
+    both("h", 2)
     for row in range(3):
         value = jnp.concatenate([pair_grads[0][row], pair_grads[1][row]], axis=1)
         vec_part[row + 1 : row + 2, :] = jnp.concatenate(
@@ -1161,23 +1340,35 @@
     unit_rows((1 - y) * 2 + (1 - c))
     send(("uc", 1), tokens.at[(1 - y) * 2 + (1 - c)], unit_core.at[1], core_dev)
     far_member = (1 - y) * 2 + c
+    sum_step(0, 0)
     unit_rows(far_member)
     recv(("uc", 1))
     tokens[far_member] = (tokens[far_member].astype(F32) + unit_core[1].astype(F32)).astype(BF16)
     send("uy", tokens.at[far_member], unit_far, y_dev)
+    both("h", 3)
+    scatter_last("h")
+    sum_step(0, 1)
     unit_rows(y * 2 + (1 - c))
     send(("uc", 0), tokens.at[y * 2 + (1 - c)], unit_core.at[0], core_dev)
+    both("o", 0)
     unit_rows(s)
     recv(("uc", 0))
-    qkv_z(0, 3)
-    scatter_near("o")
-    scatter_z("h")
-    scatter_sum("b")
+    sum_step(0, 2)
+    both("o", 1)
+    direct_start(1)
+    sum_step(0, 3)
     qkv_sum_pair(0)
-    scatter_z("o")
-    qkv_z(1, 1)
-    scatter_sum("h")
+    both("o", 2)
     recv("uy")
+
+    def unpack(p):
+        recv(("ph", p))
+        for index, ref in enumerate((gq_ref, gk_ref, gv_ref)):
+            for member in range(4):
+                first = MINE * member + PAIR * p
+                ref[:, first : first + PAIR] = qkv_home[
+                    p, member, :, PAIR * index : PAIR * (index + 1)
+                ].astype(F32)
 
     def input_back(step, carry):
         rows = tile(step, 64)
@@ -1193,59 +1384,64 @@
         return carry
 
     lax.fori_loop(0, ROWS // 64, input_back, 0)
+    results.start(ig_ref, ig_hbm)
+    links.group("sg", vec_in.at[pl.ds(0, 3)])
     for k, device in ((2, y_dev), (3, yc_dev), (1, core_dev)):
-        send(("sg", k), vec_part, vec_in.at[k - 1], device)
-    qkv_z(1, 2)
-    recv(("sg", 1), ("sg", 2), ("sg", 3))
-    links.sent(("sg", 1), ("sg", 2), ("sg", 3))
+        send(None, vec_part, vec_in.at[k - 1], device, "sg")
+    scatter_sum("b")
+    scatter_sum("h")
+    recv("sg")
+    links.sent("sg")
     vec_part[...] += vec_in[0] + vec_in[1] + vec_in[2]
     send("sx", vec_part, vec_in.at[3], x_dev)
-    qkv_z(1, 3)
-    scatter_sum("o")
+    both("o", 3)
+    scatter_last("o")
     recv("sx")
     links.sent("sx")
     vec_part[...] += vec_in[3]
+    links.group("sz", vec_in.at[pl.ds(4, 3)])
     for k in (1, 2, 3):
-        send(("sz", k), vec_part, vec_in.at[3 + k], z_devs[k])
+        send(None, vec_part, vec_in.at[3 + k], z_devs[k], "sz")
+    scatter_done("b")
+    scatter_done("h")
     qkv_sum_pair(1)
-    recv(("sz", 1), ("sz", 2), ("sz", 3))
+    scatter_sum("o")
+    unpack(0)
+    recv("sz")
     total = vec_part[...] + vec_in[4] + vec_in[5] + vec_in[6]
     gvec_ref[...] = pltpu.roll(total, WIDTH - (d * 4 + s) * SHARE, 1)[:, :128]
-    for m in "bho":
-        scatter_done(m)
-    for p in range(2):
-        recv(("ph", p, 1), ("ph", p, 2), ("ph", p, 3))
-        for index, ref in enumerate((gq_ref, gk_ref, gv_ref)):
-            for member in range(4):
-                first = MINE * member + PAIR * p
-                ref[:, first : first + PAIR] = qkv_home[
-                    p, member, :, PAIR * index : PAIR * (index + 1)
-                ].astype(F32)
+    results.start(gvec_ref, gvec_hbm)
+    scatter_done("o")
+    unpack(1)
+    for held, target in ((gq_ref, gq_hbm), (gk_ref, gk_hbm), (gv_ref, gv_hbm)):
+        results.start(held, target)
+    results.wait()
     links.sent_all()
     line_sent(("o", 0))
     line_sent(("o", 1))
-    for p in range(2):
-        line_sent(p)
-        for i in range(4):
-
-            @pl.when(s != i)
-            def _():
-                mix_copy(p, i, s).wait_send()
+    for stream in streams:
+        sum_sent(stream)
+    line_sent(0)
+    line_sent(1)
 
 
 def finish_kernel(*refs):
-    sources, gvec, targets, held, sems = refs[:8], refs[8], refs[9:22], refs[22:30], refs[30]
+    sources, gvec, targets, held = refs[:8], refs[8], refs[9:22], refs[22:30]
+    vectors, sems = refs[30:35], refs[35]
     places = (1, 0, 3, 6, 7, 9, 11, 12)
+    rows = (2, 4, 5, 8, 10)
     loads = [pltpu.make_async_copy(sources[i], held[i], sems.at[0, i]) for i in range(8)]
     stores = [pltpu.make_async_copy(held[i], targets[places[i]], sems.at[1, i]) for i in range(8)]
+    small = [pltpu.make_async_copy(vectors[i], targets[rows[i]], sems.at[1, 8 + i]) for i in range(5)]
     for copy in loads:
         copy.start()
-    for row, place in enumerate((2, 4, 5, 8, 10)):
-        targets[place][...] = gvec[row, :SHARE]
+    for row in range(5):
+        vectors[row][...] = gvec[row, :SHARE]
+        small[row].start()
     for load, store in zip(loads, stores):
         load.wait()
         store.start()
-    for copy in stores:
+    for copy in stores + small:
         copy.wait()
 
 
@@ -1272,14 +1468,20 @@
     vmem = pl.BlockSpec(memory_space=pltpu.VMEM)
     whole = (4, 2, 4 * SHARE, WIDTH)
     buffers = [
+        ((ROWS, WIDTH), BF16),
+        ((ROWS, WIDTH), F32),
+        ((8, 128), F32),
+    ]
+    buffers += [((SHARE, WIDTH), F32)] * 6
+    buffers += [
         (whole, BF16),
         (whole, BF16),
         (whole, BF16),
         (whole, BF16),
         ((3, 2, 2, 4, 2 * SHARE, WIDTH // 2), BF16),
-        ((3, 2, 4, 2 * SHARE, WIDTH // 2), BF16),
-        ((3, 4, 2 * SHARE, WIDTH // 2), BF16),
-        ((3, 3, 2 * SHARE, WIDTH // 2), BF16),
+        ((6, 4, 2 * SHARE, WIDTH // 2), BF16),
+        ((2, 6, 3, 2 * SHARE, WIDTH // 2), BF16),
+        ((3, 2 * SHARE, WIDTH // 2), BF16),
         ((2, 8, 4 * SHARE, PACK), BF16),
         ((2, 4, SHARE, PACK), BF16),
         ((4, ROWS, WIDTH), BF16),
@@ -1298,18 +1500,16 @@
         ((ROWS, WIDTH), BF16),
         ((ROWS, WIDTH), BF16),
         ((4, MINE, ROWS), BF16),
-        ((4, MINE, ROWS), BF16),
         ((ROWS, WIDTH), BF16),
         ((SLOTS, HEAD_DIM), F32),
         ((SLOTS, HEAD_DIM), F32),
-        ((MINE, SLOTS), F32),
+        ((PAIR, SLOTS), F32),
         ((2, SLOTS, PACK), BF16),
         ((2, ROWS, WIDTH), BF16),
         ((ROWS, WIDTH), BF16),
         ((2, 4, 2, 4 * SHARE, PACK), BF16),
         ((2, 4, 4 * SHARE, PACK), BF16),
-        ((2, 3, 4 * SHARE, PACK), BF16),
-        ((2, 4, SHARE, PACK), BF16),
+        ((2, 2, 3, 4 * SHARE, PACK), BF16),
         ((2, 4, SHARE, PACK), BF16),
         ((2, 2, 4, 2, 8, 128), F32),
         ((8, WIDTH + 128), F32),
@@ -1321,8 +1521,10 @@
         ((3, SHARE, WIDTH // 2), F32),
     ]
     scratch = [pltpu.VMEM(shape, kind) for shape, kind in buffers]
-    scratch += [pltpu.SemaphoreType.DMA((2, 4))] * 2 + [pltpu.SemaphoreType.DMA((3, 8, 4))] * 2
-    scratch += [pltpu.SemaphoreType.DMA((COPIES,))] * 2
+    scratch += [pltpu.SemaphoreType.DMA((9,))]
+    dma = pltpu.SemaphoreType.DMA
+    scratch += [dma, dma] + [dma((3, 8)), dma((2, 8, 3))] * 2 + [dma((2, 8))]
+    scratch += [dma((COPIES,))] * 2
     square = jax.ShapeDtypeStruct((SHARE, WIDTH), F32)
     results = pl.pallas_call(
         layer_kernel,
@@ -1338,7 +1540,7 @@
             square,
         ),
         in_specs=[vmem, pl.BlockSpec(memory_space=pltpu.SMEM)] + [vmem] * 8,
-        out_specs=tuple([vmem] * 9),
+        out_specs=tuple([pl.BlockSpec(memory_space=pl.ANY)] * 9),
         scratch_shapes=scratch,
         compiler_params=pltpu.CompilerParams(
             collective_id=0, has_side_effects=True, vmem_limit_bytes=66 * 1000 * 1000
@@ -1366,9 +1568,10 @@
         finish_kernel,
         out_shape=tuple(shapes),
         in_specs=[anywhere] * 8 + [vmem],
-        out_specs=tuple(vmem if shape is vector else anywhere for shape in shapes),
+        out_specs=tuple([anywhere] * 13),
         scratch_shapes=[pltpu.VMEM(array.shape, array.dtype) for array in moved]
-        + [pltpu.SemaphoreType.DMA((2, 8))],
+        + [pltpu.VMEM((SHARE,), F32)] * 5
+        + [pltpu.SemaphoreType.DMA((2, 13))],
         compiler_params=pltpu.CompilerParams(vmem_limit_bytes=66 * 1000 * 1000),
     )(*moved, gvec)
     return (done[0].reshape(inputs.shape), done[1].reshape(inputs.shape), *done[2:])

time: 194 us -> 183 us (0.943)
  Pallas kernels: 191 us -> 178 us
    pallas_call x1, Pallas kernels: 186 us -> 174 us  [fused_shards(): pl.pallas_call(layer_kernel, out_shape=(jax.ShapeDtypeStruct((ROWS, WIDTH...]
where the time goes in v3:
time: 183 us; the launch traced here: 181 us
  Pallas kernels  178 us (97%)
    pallas_call x1, Pallas kernels, fused_shards(): pl.pallas_call(layer_kernel, out_shape=(jax.ShapeDtypeStruct((ROWS, WIDTH...  174 us
    pallas_call x1, Pallas kernels, fused_shards(): pl.pallas_call(finish_kernel, out_shape=tuple(shapes), in_specs=[anywhere...  3.91 us

profile of v3, /device:TPU:0, one launch (start us, length us, event | category | flops | bytes accessed | tf_op | source)
XLA Modules:
  0.0 180.9 jit_solution(16490592461958710471)
XLA Ops:
  1.3 1.3 convert_add_fusion.vec_ref
  2.6 174.1 %shard_map.237 = (bf16[256,1280]{1,0:T(8,128)(2,1)}, f32[256,1280]{1,0:T(8,128)}, f32[8,128]{1,0:T(8,128)}, f32[40,1280]{1,0:T(8,128)}, f32[40,1280]{1,0:T(8,128...) custom-call(bf16[256,1280]{1,0:T(8,128)(2,1)} %bitcast.15, ...), custom_call_target="tpu_custom_call" | custom-call | flops 24999999488 | bytes 10000000 | tf_op jit(solution)/shard_map/pallas_call | solution.py:1529
  176.8 3.9 %shard_map.238 = (bf16[256,1280]{1,0:T(8,128)(2,1)}, f32[256,1280]{1,0:T(8,128)}, f32[40]{0:T(128)}, f32[40,1280]{1,0:T(8,128)}, f32[40]{0:T(128)}, /*index=5*/f...) custom-call(f32[256,1280]{1,0:T(8,128)} %get-tuple-element.35.refs_0, ...), custom_call_target="tpu_custom_call" | custom-call | tf_op jit(solution)/shard_map/pallas_call | solution.py:1567

commit v4 on v3

--- a/solution.py
+++ b/solution.py
@@ -1022,9 +1022,32 @@
         for zz in (3, 0, 2, 1):
             sum_copy(2, stream, zz).start()
 
+    def near_copy(zz):
+        return pltpu.make_async_remote_copy(
+            src_ref=sum_piece(("o", 1), zz, 0),
+            dst_ref=line_in.at[zz // 3, 1, zz % 3],
+            send_sem=sum_send.at[0, 3],
+            recv_sem=sum_recv.at[0, 3, 0],
+            device_id=devs_of(last_x["o"])[0],
+            device_id_type=MESH_ID,
+        )
+
+    def cross():
+        add_far(("o", 1))
+        for zz in (3, 0, 2, 1):
+            near_copy(zz).start()
+
+    def add_near():
+        pieces(("o", 1), 4, sum_send.at[0, 3], sum_recv.at[0, 3, 0]).wait_recv()
+        for zz in range(4):
+            piece = sum_piece(("o", 0), zz, 0)
+            piece[...] = (piece[...].astype(F32) + line_in[zz // 3, 1, zz % 3].astype(F32)).astype(BF16)
+
     def sum_step(stream, step):
         if step == 0:
             add_far(stream)
+            if stream == ("o", 0):
+                add_near()
         above, below = z + 3 - step, z + step - 3
 
         @pl.when((z >= 1) & (z <= step))
@@ -1056,7 +1079,7 @@
                 for zz in (0, 1, 2):
                     sum_copy(1, stream, zz).start()
 
-    direct = (1,)
+    direct = (1, ("o", 0),)
 
     def direct_copy(stream, k):
         index = streams.index(stream)
@@ -1071,6 +1094,8 @@
 
     def direct_start(stream):
         add_far(stream)
+        if stream == ("o", 0):
+            add_near()
         for k in (2, 1, 3):
             direct_copy(stream, k).start()
 
@@ -1085,7 +1110,9 @@
     def sum_sent(stream):
         index = streams.index(stream)
         recvs = far_recv.at[1, index]
-        if stream in direct:
+        if stream == ("o", 1):
+            pieces(stream, 4, sum_send.at[0, index], recvs).wait_send()
+        elif stream in direct:
             pieces(stream, 3, sum_send.at[0, index], recvs).wait_send()
         else:
             for zz in range(3):
@@ -1126,20 +1153,24 @@
     def scatter_far(m):
         for e in (0, 1):
             core_add(m, 1, e)
+        for e in (1, 0) if m == "o" else (0, 1):
             sum_far((m, e))
         for e in (0, 1):
             core_add(m, 0, e)
 
     def both(m, step):
         sum_step((m, 0), step)
-        sum_step((m, 1), step)
+        if m != "o":
+            sum_step((m, 1), step)
 
     def scatter_last(m):
         send(("gl", m), sum_piece((m, 1), z, 0), last_in.at[order[m]], devs_of(last_x[m])[0])
 
     def scatter_sum(m):
-        recv(("gl", m))
-        total = sum_piece((m, 0), z, 0)[...].astype(F32) + last_in[order[m]].astype(F32)
+        total = sum_piece((m, 0), z, 0)[...].astype(F32)
+        if m != "o":
+            recv(("gl", m))
+            total += last_in[order[m]].astype(F32)
         outs[m][:, half(c)] = jnp.where(c == 0, total[:SHARE], total[SHARE:])
         give_out[order[m]] = jnp.where(c == 0, total[SHARE:], total[:SHARE])
         send(("give", m), give_out.at[order[m]], give_in.at[order[m]], core_dev)
@@ -1350,15 +1381,14 @@
     sum_step(0, 1)
     unit_rows(y * 2 + (1 - c))
     send(("uc", 0), tokens.at[y * 2 + (1 - c)], unit_core.at[0], core_dev)
-    both("o", 0)
+    cross()
     unit_rows(s)
     recv(("uc", 0))
     sum_step(0, 2)
-    both("o", 1)
     direct_start(1)
     sum_step(0, 3)
     qkv_sum_pair(0)
-    both("o", 2)
+    direct_start(("o", 0))
     recv("uy")
 
     def unpack(p):
@@ -1394,8 +1424,6 @@
     links.sent("sg")
     vec_part[...] += vec_in[0] + vec_in[1] + vec_in[2]
     send("sx", vec_part, vec_in.at[3], x_dev)
-    both("o", 3)
-    scatter_last("o")
     recv("sx")
     links.sent("sx")
     vec_part[...] += vec_in[3]
@@ -1405,6 +1433,7 @@
     scatter_done("b")
     scatter_done("h")
     qkv_sum_pair(1)
+    direct_done(("o", 0))
     scatter_sum("o")
     unpack(0)
     recv("sz")

time: 183 us -> 179 us (0.978); the launches traced: 181 us -> 179 us
  Pallas kernels: 178 us -> 176 us
    pallas_call x1, Pallas kernels: 174 us -> 172 us  [fused_shards(): pl.pallas_call(layer_kernel, out_shape=(jax.ShapeDtypeStruct((ROWS, WIDTH...]
where the time goes in v4:
time: 179 us
  Pallas kernels  176 us (98%)
    pallas_call x1, Pallas kernels, fused_shards(): pl.pallas_call(layer_kernel, out_shape=(jax.ShapeDtypeStruct((ROWS, WIDTH...  172 us
    pallas_call x1, Pallas kernels, fused_shards(): pl.pallas_call(finish_kernel, out_shape=tuple(shapes), in_specs=[anywhere...  3.91 us

profile of v4, /device:TPU:0, one launch (start us, length us, event | category | flops | bytes accessed | tf_op | source)
XLA Modules:
  0.0 178.9 jit_solution(5374900613485048149)
XLA Ops:
  1.3 1.3 convert_add_fusion.vec_ref
  2.6 172.2 %shard_map.237 = (bf16[256,1280]{1,0:T(8,128)(2,1)}, f32[256,1280]{1,0:T(8,128)}, f32[8,128]{1,0:T(8,128)}, f32[40,1280]{1,0:T(8,128)}, f32[40,1280]{1,0:T(8,128...) custom-call(bf16[256,1280]{1,0:T(8,128)(2,1)} %bitcast.15, ...), custom_call_target="tpu_custom_call" | custom-call | flops 24999999488 | bytes 10000000 | tf_op jit(solution)/shard_map/pallas_call | solution.py:1558
  174.8 3.9 %shard_map.238 = (bf16[256,1280]{1,0:T(8,128)(2,1)}, f32[256,1280]{1,0:T(8,128)}, f32[40]{0:T(128)}, f32[40,1280]{1,0:T(8,128)}, f32[40]{0:T(128)}, /*index=5*/f...) custom-call(f32[256,1280]{1,0:T(8,128)} %get-tuple-element.35.refs_0, ...), custom_call_target="tpu_custom_call" | custom-call | tf_op jit(solution)/shard_map/pallas_call | solution.py:1596

commit v5 on v4

--- a/solution.py
+++ b/solution.py
@@ -461,7 +461,11 @@
     x_ref,
     len_ref,
     cot_ref,
-    vec_ref,
+    gain_ref,
+    query_bias_ref,
+    query_scale_ref,
+    value_bias_ref,
+    gain_mlp_ref,
     wq_ref,
     wk_ref,
     wv_ref,
@@ -480,6 +484,7 @@
     out_ref,
     ig_ref,
     gvec_ref,
+    vec_ref,
     gq_ref,
     gk_ref,
     gv_ref,
@@ -571,6 +576,9 @@
     for p in range(2):
         qkv_own[p, s] = stage[p, s]
     tokens[s] = x_ref[...]
+    vec_ref[...] = jnp.zeros_like(vec_ref)
+    for row, ref in enumerate((gain_ref, query_bias_ref, query_scale_ref, value_bias_ref, gain_mlp_ref)):
+        vec_ref[row : row + 1, :SHARE] = ref[...].astype(F32)
     vec_slots[y, x, z, c] = vec_ref[...]
     shards = {"o": wo_ref, "h": wh_ref, "b": wb_ref}
     slot_of = {"o": 0, "h": 1, "b": 2}
@@ -1348,8 +1356,8 @@
     recv(("gm", 1))
     attend_back(2)
     attend_back(3)
+    pair_grads.append(finish_pair(1))
     both("h", 1)
-    pair_grads.append(finish_pair(1))
     qkv_grad_pair(1)
     both("h", 2)
     for row in range(3):
@@ -1490,15 +1498,13 @@
     w_hidden,
     w_back,
 ):
-    vectors = sum(
-        jnp.pad(value.astype(F32)[None], ((row, 7 - row), (0, 128 - SHARE)))
-        for row, value in enumerate((gain_attn, bias_query, query_scale, bias_value, gain_mlp))
-    )
+    vectors = [v.reshape(1, SHARE) for v in (gain_attn, bias_query, query_scale, bias_value, gain_mlp)]
     vmem = pl.BlockSpec(memory_space=pltpu.VMEM)
     whole = (4, 2, 4 * SHARE, WIDTH)
     buffers = [
         ((ROWS, WIDTH), BF16),
         ((ROWS, WIDTH), F32),
+        ((8, 128), F32),
         ((8, 128), F32),
     ]
     buffers += [((SHARE, WIDTH), F32)] * 6
@@ -1568,7 +1574,7 @@
             square,
             square,
         ),
-        in_specs=[vmem, pl.BlockSpec(memory_space=pltpu.SMEM)] + [vmem] * 8,
+        in_specs=[vmem, pl.BlockSpec(memory_space=pltpu.SMEM)] + [vmem] * 12,
         out_specs=tuple([pl.BlockSpec(memory_space=pl.ANY)] * 9),
         scratch_shapes=scratch,
         compiler_params=pltpu.CompilerParams(
@@ -1579,7 +1585,7 @@
         inputs.reshape(ROWS, WIDTH),
         lengths,
         cotangent.reshape(ROWS, WIDTH),
-        vectors,
+        *vectors,
         w_query,
         w_key,
         w_value,

time: 179 us -> 178 us (level)
  no operation moved by 1% of the time
where the time goes in v5:
time: 178 us; the launch traced here: 177 us
  Pallas kernels  176 us (99%)
    pallas_call x1, Pallas kernels, fused_shards(): pl.pallas_call(layer_kernel, out_shape=(jax.ShapeDtypeStruct((ROWS, WIDTH...  172 us
    pallas_call x1, Pallas kernels, fused_shards(): pl.pallas_call(finish_kernel, out_shape=tuple(shapes), in_specs=[anywhere...  3.91 us

profile of v5, /device:TPU:0, one launch (start us, length us, event | category | flops | bytes accessed | tf_op | source)
XLA Modules:
  0.0 177.4 jit_solution(7386903261765385688)
XLA Ops:
  1.3 172.0 %shard_map.237 = (bf16[256,1280]{1,0:T(8,128)(2,1)}, f32[256,1280]{1,0:T(8,128)}, f32[8,128]{1,0:T(8,128)}, f32[40,1280]{1,0:T(8,128)}, f32[40,1280]{1,0:T(8,128...) custom-call(bf16[256,1280]{1,0:T(8,128)(2,1)} %bitcast.10, ...), custom_call_target="tpu_custom_call" | custom-call | flops 24999999488 | bytes 10000000 | tf_op jit(solution)/shard_map/pallas_call | solution.py:1564
  173.3 3.9 %shard_map.238 = (bf16[256,1280]{1,0:T(8,128)(2,1)}, f32[256,1280]{1,0:T(8,128)}, f32[40]{0:T(128)}, f32[40,1280]{1,0:T(8,128)}, f32[40]{0:T(128)}, /*index=5*/f...) custom-call(f32[256,1280]{1,0:T(8,128)} %get-tuple-element.35.refs_0, ...), custom_call_target="tpu_custom_call" | custom-call | tf_op jit(solution)/shard_map/pallas_call | solution.py:1602
